TPU v7x, 32 devices: a whole 2x2x4 slice. The times are simulated.
32 devices in a mesh: groups: 2 (over y), blocks: 4 (over z), dp: 2 (over x), sub: 2 (over core).
Axes of the slice: x: 2, y: 2, z: 4, core: 2. Of those that a mesh axis runs over, the one named last changes fastest.
Arguments:
- features: bfloat16 [8, 96, 2048], P(('groups', 'dp', 'sub'), None, 'blocks'), parts along dimension 0, may hold values from -6 to 6
- grad_out: bfloat16 [8, 96, 2048], P(('groups', 'dp', 'sub'), None, 'blocks'), parts along dimension 0, may hold values from -6 to 6
- weight_one: bfloat16 [96, 2592], replicated, may hold values from -0.21875 to 0.21875
- weight_two: bfloat16 [96, 2592], replicated, may hold values from -0.21875 to 0.21875
- bias_one: float32 [96], replicated, may hold values from -3 to 3
- bias_two: float32 [96], replicated, may hold values from -3 to 3
- heights: int32 [8, 16, 64], P(('groups', 'dp', 'sub'), 'blocks'), parts along dimension 0, may hold values from 2 to 4
- counts: int32 [8, 16, 64], P(('groups', 'dp', 'sub'), 'blocks'), parts along dimension 0, may hold values from 1 to 2
- neighbours: int32 [8, 16, 8], P(('groups', 'dp', 'sub'), 'blocks'), parts along dimension 0, may hold values from -1 to 15, as said below
Outputs:
- out_features: bfloat16 [8, 96, 2048], P(('groups', 'dp', 'sub'), None, 'blocks'), parts along dimension 0
- input_grad: bfloat16 [8, 96, 2048], P(('groups', 'dp', 'sub'), None, 'blocks'), parts along dimension 0
- weight_one_grad: float32 [192, 2592], P('groups'), parts along dimension 0
- weight_two_grad: float32 [192, 2592], P('groups'), parts along dimension 0
- bias_one_grad: float32 [192], P('groups'), parts along dimension 0
- bias_two_grad: float32 [192], P('groups'), parts along dimension 0
There are 2 independent parts, one for each index of `groups`. A program takes and returns all parts, laid end to end along the dimension named above; an argument that names none is the same for every part. Nothing has to cross between parts.
Inputs may be any that keep to these rules, and one draw needn't show every extreme that they name: A global slot is the device index along blocks times 4 plus the local slot. Each region is a sheet of 4 by 4 blocks cut into tiles of 2 x 2 blocks, on a grid of 2 rows and 2 columns of tiles; a device holds one tile of each of its 1 regions (local slot 4 r + 2 i + j is block (i, j) of the tile of region r). The tile in row a and column b of a region lies on the device (start + 2 a + b) mod 4, with a start drawn for each region. The relation is symmetric and geometric, and neighbours never cross regions.
All inputs are finite; a program needn't handle non-finite values.
Results may differ from a plain program's by a relative error of at most 0.006.
Values may be sent and summed in bfloat16 or wider, within the bound.
A program may use at most 64 MiB of HBM per device.

v0:
```python
import jax
import jax.numpy as jnp
import numpy as np
from jax import lax
from jax.sharding import PartitionSpec as P

C = 96
SIDE = 8
KMAX = 2


DIRECTIONS = ((1, 0), (-1, 0), (0, 1), (0, -1), (1, 1), (1, -1), (-1, 1), (-1, -1))
OPPOSITE = (1, 0, 3, 2, 7, 6, 5, 4)
CLASSES = ((0, 1), (0, -1), (1, 0), (1, 1), (1, -1))
SHIFTS = np.array(
    [
        [vertical, across, along]
        for vertical in (-1, 0, 1)
        for across in (-1, 0, 1)
        for along in (-1, 0, 1)
    ],
    np.int32,
)


def as_sent(array):

    def short(part):
        return part.astype(jnp.bfloat16) if part.dtype == jnp.float32 else part

    return jax.tree.map(short, array)


def shifted(block, axis, distance):
    devices = range(lax.axis_size(axis))
    route = [((i - distance) % len(devices), i) for i in devices]
    return lax.ppermute(block, axis, route)


def silu_slope(values):
    squash = jax.nn.sigmoid(values)
    return squash * (1.0 + values * (1.0 - squash))


def span_range(step, halo_depth, side):
    if step > 0:
        return range(side - halo_depth, side)
    if step < 0:
        return range(0, halo_depth)
    return range(0, side)


def box_columns(direction, halo_depth, side):
    step_x, step_y = DIRECTIONS[direction]
    return [
        (across, along)
        for across in span_range(step_x, halo_depth, side)
        for along in span_range(step_y, halo_depth, side)
    ]


def grid_layout(halo_depth, side):
    direction_codes = []
    columns = []
    places = []
    for grid_x in range(-halo_depth, side + halo_depth):
        for grid_y in range(-halo_depth, side + halo_depth):
            step_x = int(grid_x >= side) - int(grid_x < 0)
            step_y = int(grid_y >= side) - int(grid_y < 0)
            source_x = grid_x - side * step_x
            source_y = grid_y - side * step_y
            if step_x == 0 and step_y == 0:
                direction_codes.append(-1)
                places.append(0)
            else:
                code_here = DIRECTIONS.index((step_x, step_y))
                direction_codes.append(code_here)
                places.append(
                    box_columns(OPPOSITE[code_here], halo_depth, side).index((source_x, source_y))
                )
            columns.append(source_x * side + source_y)
    return (
        np.array(direction_codes, np.int32),
        np.array(columns, np.int32),
        np.array(places, np.int32),
    )


def class_units():
    result = []
    for across_flag, column_step in CLASSES:
        face_units = []
        edge_units = []
        for block in range(4):
            row_bit = block // 2
            col_bit = block % 2
            for direction in range(8):
                step_x, step_y = DIRECTIONS[direction]
                tile_x = (row_bit + step_x) // 2
                tile_y = (col_bit + step_y) // 2
                if int(tile_x != 0) == across_flag and tile_y == column_step:
                    if direction < 4:
                        face_units.append((block, direction))
                    else:
                        edge_units.append((block, direction))
        result.append((face_units, edge_units))
    return result


def class_columns(halo_depth, regions):
    lists = []
    for face_units, edge_units in class_units():
        picked = []
        for region in range(regions):
            for block, direction in face_units + edge_units:
                for across, along in box_columns(direction, halo_depth, SIDE):
                    picked.append((4 * region + block) * SIDE * SIDE + across * SIDE + along)
        lists.append(np.array(picked, np.int32))
    return lists


def class_offsets(parties):
    half = parties // 2
    return [(across_flag * half + column_step) % parties for across_flag, column_step in CLASSES]


def move_rows(own_rows, halo_depth, parties, mover):
    slot_count = own_rows.shape[1] // (SIDE * SIDE * KMAX)
    arrived = []
    for column_list, offset in zip(
        class_columns(halo_depth, slot_count // 4), class_offsets(parties)
    ):
        row_index = (
            column_list[:, None] * KMAX + np.arange(KMAX, dtype=np.int32)[None, :]
        ).reshape(-1)
        arrived.append(mover(jnp.take(own_rows, row_index, axis=1), offset))
    padding = jnp.zeros((C, KMAX), jnp.bfloat16)
    return jnp.concatenate([own_rows] + arrived + [padding], axis=1)


def move_levels(own_heights, own_counts, halo_depth, parties, mover):
    slot_count = own_heights.shape[0]
    stacked = jnp.stack([own_heights.reshape(-1), own_counts.reshape(-1)]).astype(jnp.int32)
    arrived = []
    for column_list, offset in zip(
        class_columns(halo_depth, slot_count // 4), class_offsets(parties)
    ):
        arrived.append(mover(stacked[:, column_list], offset))
    table = jnp.concatenate([stacked] + arrived + [jnp.zeros((2, 1), jnp.int32)], axis=1)
    return (table[0], table[1])


def grid_ids(neighbours, halo_depth, slot_count):
    regions = slot_count // 4
    direction_codes, columns, places = grid_layout(halo_depth, SIDE)
    units = class_units()
    own_count = slot_count * SIDE * SIDE
    widths = [
        len(face_units) * halo_depth * SIDE + len(edge_units) * halo_depth * halo_depth
        for face_units, edge_units in units
    ]
    class_starts = own_count + regions * np.cumsum([0] + widths[:-1])
    zero_column = own_count + regions * sum(widths)
    base = np.zeros((4, len(columns)), np.int64)
    stride = np.zeros((4, len(columns)), np.int64)
    for block in range(4):
        row_bit = block // 2
        col_bit = block % 2
        for spot in range(len(columns)):
            code_here = int(direction_codes[spot])
            if code_here < 0:
                base[block, spot] = block * SIDE * SIDE + columns[spot]
                stride[block, spot] = 4 * SIDE * SIDE
                continue
            step_x, step_y = DIRECTIONS[code_here]
            tile_x = (row_bit + step_x) // 2
            tile_y = (col_bit + step_y) // 2
            other = 2 * ((row_bit + step_x) % 2) + (col_bit + step_y) % 2
            if tile_x == 0 and tile_y == 0:
                base[block, spot] = other * SIDE * SIDE + columns[spot]
                stride[block, spot] = 4 * SIDE * SIDE
            else:
                number = CLASSES.index((int(tile_x != 0), -tile_y))
                face_units, edge_units = units[number]
                unit = (other, OPPOSITE[code_here])
                if code_here < 4:
                    inner = face_units.index(unit) * halo_depth * SIDE
                else:
                    inner = (
                        len(face_units) * halo_depth * SIDE
                        + edge_units.index(unit) * halo_depth * halo_depth
                    )
                base[block, spot] = class_starts[number] + inner + places[spot]
                stride[block, spot] = widths[number]
    slot_numbers = np.arange(slot_count)
    static_ids = (
        base[slot_numbers % 4] + (slot_numbers // 4)[:, None] * stride[slot_numbers % 4]
    ).astype(np.int32)
    nearby = neighbours[:, np.maximum(direction_codes, 0)]
    exists = (direction_codes[None, :] < 0) | (nearby >= 0)
    return (jnp.where(exists, jnp.asarray(static_ids), zero_column).astype(jnp.int32), zero_column)


def conv_index(grid_heights, grid_counts, grid_idents, halo_depth, out_depth, zero_row):
    grid_width = SIDE + 2 * halo_depth
    out_width = SIDE + 2 * out_depth
    margin = halo_depth - out_depth
    spots = np.arange(out_width, dtype=np.int32) + margin
    centre = (spots[:, None] * grid_width + spots[None, :]).reshape(-1)
    source = (
        (spots[None, :, None] + SHIFTS[:, 1][:, None, None]) * grid_width
        + spots[None, None, :]
        + SHIFTS[:, 2][:, None, None]
    ).reshape(27, -1)
    own_heights = grid_heights[:, centre]
    own_counts = grid_counts[:, centre]
    source_heights = grid_heights[:, source]
    source_counts = grid_counts[:, source]
    source_ids = grid_idents[:, source]
    layers = jnp.arange(KMAX, dtype=jnp.int32)[:, None, None, None]
    level_index = (
        own_heights[None, :, None, :]
        + layers
        + SHIFTS[:, 0][None, None, :, None]
        - source_heights[None]
    )
    row_live = layers < own_counts[None, :, None, :]
    present = row_live & (level_index >= 0) & (level_index < source_counts[None])
    picked = jnp.where(present, source_ids[None] * KMAX + level_index, zero_row)
    gather_index = jnp.transpose(picked, (2, 1, 3, 0)).reshape(27, -1).astype(jnp.int32)
    live_kmax = jnp.arange(KMAX, dtype=jnp.int32)[:, None, None] < own_counts[None]
    live_rows = jnp.transpose(live_kmax, (1, 2, 0)).reshape(-1)
    return (gather_index, live_rows)


def convolve(source_table, gather_index, weights):
    kernel = weights.reshape(C, C, 27)
    running = jnp.zeros((C, gather_index.shape[1]), jnp.float32)
    for group_number in range(3):
        gathered = jnp.take(
            source_table, gather_index[9 * group_number : 9 * group_number + 9], axis=1
        )
        running = running + jnp.einsum(
            "oik,ikr->or",
            kernel[:, :, 9 * group_number : 9 * group_number + 9],
            gathered,
            preferred_element_type=jnp.float32,
        )
    return running


def convolve_back(source_table, gather_index, weights):
    kernel = weights.reshape(C, C, 27)
    flipped = gather_index[::-1]
    running = jnp.zeros((C, gather_index.shape[1]), jnp.float32)
    for group_number in range(3):
        gathered = jnp.take(source_table, flipped[9 * group_number : 9 * group_number + 9], axis=1)
        running = running + jnp.einsum(
            "oik,okr->ir",
            kernel[:, :, 9 * group_number : 9 * group_number + 9],
            gathered,
            preferred_element_type=jnp.float32,
        )
    return running


def kernel_grad(source_table, gather_index, gradients):
    pieces = []
    for group_number in range(3):
        gathered = jnp.take(
            source_table, gather_index[9 * group_number : 9 * group_number + 9], axis=1
        )
        pieces.append(
            jnp.einsum("or,ikr->oik", gradients, gathered, preferred_element_type=jnp.float32)
        )
    return jnp.concatenate(pieces, axis=2).reshape(C, C * 27)


def send_input(values, offset):
    return jax.tree.map(
        lambda part, own: part.astype(own.dtype), shifted(as_sent(values), "blocks", offset), values
    )


def send_levels(values, offset):
    return shifted(values, "blocks", offset)


def send_hidden(values, offset):
    return jax.tree.map(
        lambda part, own: part.astype(own.dtype), shifted(as_sent(values), "blocks", offset), values
    )


def send_grad_two(values, offset):
    return jax.tree.map(
        lambda part, own: part.astype(own.dtype), shifted(as_sent(values), "blocks", offset), values
    )


def send_grad_one(values, offset):
    return jax.tree.map(
        lambda part, own: part.astype(own.dtype), shifted(as_sent(values), "blocks", offset), values
    )


def on_device(
    features, grad_out, weight_one, weight_two, bias_one, bias_two, heights, counts, neighbours
):
    own_rows = features[0]
    upstream = grad_out[0]
    own_heights = heights[0]
    own_counts = counts[0]
    nearby_all = neighbours[0]
    slot_count = own_heights.shape[0]
    parties = lax.axis_size("blocks")
    live_rows = (np.arange(KMAX, dtype=np.int32)[None, None, :] < own_counts[:, :, None]).reshape(
        -1
    )
    live = live_rows[None, :]
    masked = jnp.where(live, own_rows, 0).astype(jnp.bfloat16)
    near_ids, near_zero = grid_ids(nearby_all, 1, slot_count)
    height_table, count_table = move_levels(own_heights, own_counts, 1, parties, send_levels)
    near_heights = height_table[near_ids]
    near_counts = count_table[near_ids]
    back_index = conv_index(near_heights, near_counts, near_ids, 1, 0, near_zero * KMAX)[0]
    input_table = move_rows(masked, 1, parties, send_input)
    pre_one = convolve(input_table, back_index, weight_one) + bias_one[:, None]
    hidden = jnp.where(live, jax.nn.silu(pre_one), 0.0).astype(jnp.bfloat16)
    hidden_table = move_rows(hidden, 1, parties, send_hidden)
    pre_two = convolve(hidden_table, back_index, weight_two) + bias_two[:, None]
    out_features = jnp.where(live, jax.nn.silu(pre_two), 0.0).astype(jnp.bfloat16)
    grad_two = jnp.where(live, upstream.astype(jnp.float32) * silu_slope(pre_two), 0.0).astype(
        jnp.bfloat16
    )
    weight_two_part = kernel_grad(hidden_table, back_index, grad_two)
    bias_two_part = jnp.sum(grad_two.astype(jnp.float32), axis=1)
    shards = parties * lax.axis_size("dp") * lax.axis_size("sub")
    grad_two_table = move_rows(grad_two, 1, parties, send_grad_two)
    hidden_sum = convolve_back(grad_two_table, back_index, weight_two)
    grad_one = jnp.where(live, hidden_sum * silu_slope(pre_one), 0.0).astype(jnp.bfloat16)
    weight_one_part = kernel_grad(input_table, back_index, grad_one)
    bias_one_part = jnp.sum(grad_one.astype(jnp.float32), axis=1)
    grad_one_table = move_rows(grad_one, 1, parties, send_grad_one)
    input_grad = jnp.where(live, convolve_back(grad_one_table, back_index, weight_one), 0.0).astype(
        jnp.bfloat16
    )
    weight_one_total, bias_one_total, weight_two_total, bias_two_total = lax.psum(
        (weight_one_part, bias_one_part, weight_two_part, bias_two_part), ("blocks", "dp", "sub")
    )
    scale = 1.0 / shards
    return (
        out_features[None],
        input_grad[None],
        weight_one_total * scale,
        weight_two_total * scale,
        bias_one_total * scale,
        bias_two_total * scale,
    )


def solution(mesh):
    placed = (
        P(("groups", "dp", "sub"), None, "blocks"),
        P(("groups", "dp", "sub"), None, "blocks"),
        P(),
        P(),
        P(),
        P(),
        P(("groups", "dp", "sub"), "blocks", None),
        P(("groups", "dp", "sub"), "blocks", None),
        P(("groups", "dp", "sub"), "blocks", None),
    )
    return jax.shard_map(
        on_device,
        mesh=mesh,
        in_specs=placed,
        out_specs=(
            P(("groups", "dp", "sub"), None, "blocks"),
            P(("groups", "dp", "sub"), None, "blocks"),
            P("groups", None),
            P("groups", None),
            P("groups"),
            P("groups"),
        ),
        check_vma=False,
    )
```

profile of v0, /device:TPU:0, one launch (start us, length us, event | category | flops | bytes accessed | tf_op | source)
XLA Modules:
  0.0 333.0 jit_solution(3331034165445272984)
XLA Ops:
  11.3 3.1 collective-permute-start.4
  15.7 2.1 collective-permute-start.3
  19.2 2.1 collective-permute-start.1
  24.1 3.8 %collective-permute-start.8 = (s32[2,2]{0,1:T(2,128)S(1)}, s32[2,2]{0,1:T(2,128)S(1)}, u32[]{:S(2)}, u32[]{:S(2)}) collective-permute-start(s32[2,2]{0,1:T(2,128)S(1)} %bitcast.283), channel_id=1, source_target_pairs={{4,0},{8,4},{12,8},{0,12},{5,1},{9,5},{13,9},{1,13},{6,2},{10,6},{... | collective-permute-start | bytes 56 | tf_op jit(solution)/shard_map/ppermute | solution.py:37
  40.0 3.3 gather_fusion.12
  44.2 3.8 %collective-permute-start.6 = (s32[2,18]{0,1:T(8,128)S(1)}, s32[2,18]{0,1:T(8,128)S(1)}, u32[]{:S(2)}, u32[]{:S(2)}) collective-permute-start(s32[2,18]{0,1:T(8,128)S(1)} %bitcast.285), channel_id=1, source_target_pairs={{4,0},{8,4},{12,8},{0,12},{5,1},{9,5},{13,9},{1,13},{6,2},{10,6},{... | collective-permute-start | bytes 440 | tf_op jit(solution)/shard_map/ppermute | solution.py:37
  50.3 4.2 %collective-permute-done.7 = s32[2,36]{0,1:T(8,128)S(1)} collective-permute-done((s32[2,36]{0,1:T(8,128)S(1)}, s32[2,36]{0,1:T(8,128)S(1)}, u32[]{:S(2)}, u32[]{:S(2)}) %collective-permute-start.7) | collective-permute-done | bytes 320 | tf_op jit(solution)/shard_map/ppermute | solution.py:37
  54.6 3.1 gather_fusion.8
  57.8 3.1 gather_fusion.6
  61.3 3.3 gather_fusion.11
  65.8 3.3 gather_fusion.10
  76.8 8.8 %gather_fusion.19 = bf16[4608,96]{1,0:T(8,128)(2,1)S(1)} fusion(bf16[96,666]{0,1:T(8,128)(2,1)S(1)} %copy.394, s32[5120]{0:T(1024)S(1)} %pad_clamp_fusion.4), kind=kCustom, calls=%fused_computation.21.clone | custom fusion | bytes 1787904 | tf_op jit(solution)/shard_map/jit(_take)/gather | solution.py:240
  86.2 8.8 %gather_fusion.18 = bf16[4608,96]{1,0:T(8,128)(2,1)S(1)} fusion(bf16[96,666]{0,1:T(8,128)(2,1)S(1)} %copy.394, s32[5120]{0:T(1024)S(1)} %pad_clamp_fusion.5), kind=kCustom, calls=%fused_computation.3.clone | custom fusion | bytes 1787904 | tf_op jit(solution)/shard_map/jit(_take)/gather | solution.py:240
  95.6 8.8 %gather_fusion.20 = bf16[4608,96]{1,0:T(8,128)(2,1)S(1)} fusion(bf16[96,666]{0,1:T(8,128)(2,1)S(1)} %copy.394, s32[5120]{0:T(1024)S(1)} %pad_clamp_fusion.3), kind=kCustom, calls=%fused_computation.22.clone | custom fusion | bytes 1787904 | tf_op jit(solution)/shard_map/jit(_take)/gather | solution.py:240
  113.1 3.6 %collective-permute-start.13 = (bf16[96,4]{1,0:T(8,128)(2,1)S(1)}, bf16[96,4]{1,0:T(8,128)(2,1)S(1)}, u32[]{:S(2)}, u32[]{:S(2)}) collective-permute-start(bf16[96,4]{1,0:T(8,128)(2,1)S(1)} %bitcast.269), channel_id=1, source_target_pairs={{4,0},{8,4},{12,8},{0,12},{5,1},{9,5},{13,9},{1,13},{6,2},{10,6},{... | collective-permute-start | bytes 2312 | tf_op jit(solution)/shard_map/ppermute | solution.py:37
  123.8 8.8 %gather_fusion.28 = bf16[4608,96]{1,0:T(8,128)(2,1)S(1)} fusion(bf16[96,666]{0,1:T(8,128)(2,1)S(1)} %copy.419, s32[5120]{0:T(1024)S(1)} %pad_clamp_fusion.3), kind=kCustom, calls=%fused_computation.25.clone | custom fusion | bytes 1787904 | tf_op jit(solution)/shard_map/jit(_take)/gather | solution.py:240
  132.6 8.8 %gather_fusion.27 = bf16[4608,96]{1,0:T(8,128)(2,1)S(1)} fusion(bf16[96,666]{0,1:T(8,128)(2,1)S(1)} %copy.419, s32[5120]{0:T(1024)S(1)} %pad_clamp_fusion.4), kind=kCustom, calls=%fused_computation.24.clone | custom fusion | bytes 1787904 | tf_op jit(solution)/shard_map/jit(_take)/gather | solution.py:240
  141.4 10.1 %gather_fusion.26 = bf16[4608,96]{1,0:T(8,128)(2,1)} fusion(bf16[96,666]{0,1:T(8,128)(2,1)S(1)} %copy.419, s32[5120]{0:T(1024)S(1)} %pad_clamp_fusion.5), kind=kCustom, calls=%fused_computation.23.clone | custom fusion | bytes 1787904 | tf_op jit(solution)/shard_map/jit(_take)/gather | solution.py:240
  157.7 1.7 convert_reduce_fusion
  170.7 3.4 %collective-permute-start.18 = (bf16[96,4]{1,0:T(8,128)(2,1)}, bf16[96,4]{1,0:T(8,128)(2,1)}, u32[]{:S(2)}, u32[]{:S(2)}) collective-permute-start(bf16[96,4]{1,0:T(8,128)(2,1)} %bitcast.58), channel_id=1, source_target_pairs={{4,0},{8,4},{12,8},{0,12},{5,1},{9,5},{13,9},{1,13},{6,2},{10,6},{... | collective-permute-start | bytes 2312 | tf_op jit(solution)/shard_map/ppermute | solution.py:37
  182.2 8.8 %gather_fusion.36 = bf16[4608,96]{1,0:T(8,128)(2,1)S(1)} fusion(bf16[96,666]{0,1:T(8,128)(2,1)S(1)} %copy.446, s32[5120]{0:T(1024)S(1)} %pad_clamp_fusion), kind=kCustom, calls=%fused_computation.28.clone | custom fusion | bytes 1787904 | tf_op jit(solution)/shard_map/jit(_take)/gather | solution.py:257
  191.6 8.8 %gather_fusion.35 = bf16[4608,96]{1,0:T(8,128)(2,1)S(1)} fusion(bf16[96,666]{0,1:T(8,128)(2,1)S(1)} %copy.446, s32[5120]{0:T(1024)S(1)} %pad_clamp_fusion.1), kind=kCustom, calls=%fused_computation.27.clone | custom fusion | bytes 1787904 | tf_op jit(solution)/shard_map/jit(_take)/gather | solution.py:257
  201.7 8.8 %gather_fusion.34 = bf16[4608,96]{1,0:T(8,128)(2,1)S(1)} fusion(bf16[96,666]{0,1:T(8,128)(2,1)S(1)} %copy.446, s32[5120]{0:T(1024)S(1)} %pad_clamp_fusion.2), kind=kCustom, calls=%fused_computation.26.clone | custom fusion | bytes 1787904 | tf_op jit(solution)/shard_map/jit(_take)/gather | solution.py:257
  223.3 1.7 collective-permute-start.24
  225.0 2.2 collective-permute-start.23
  229.2 30.0 %all-reduce = (f32[96]{0:T(128)S(1)}, f32[96]{0:T(128)S(1)}) all-reduce(f32[96]{0:T(128)S(1)} %get-tuple-element.48, f32[96]{0:T(128)S(1)} %copy-done.63), channel_id=1, replica_groups=mesh['groups'=2,'blocks'=4,'dp'=2,'sub'=2] {'blocks','dp','sub'}, use_global_device_ids=true, to_apply=%region_3.8 | all-reduce | flops 192 | bytes 1536 | tf_op jit(solution)/shard_map/psum | solution.py:348
  260.1 8.8 %gather_fusion.44 = bf16[4608,96]{1,0:T(8,128)(2,1)S(1)} fusion(bf16[96,666]{0,1:T(8,128)(2,1)S(1)} %copy.470, s32[5120]{0:T(1024)S(1)} %pad_clamp_fusion), kind=kCustom, calls=%fused_computation.31.clone | custom fusion | bytes 1787904 | tf_op jit(solution)/shard_map/jit(_take)/gather | solution.py:257
  268.9 8.8 %gather_fusion.43 = bf16[4608,96]{1,0:T(8,128)(2,1)S(1)} fusion(bf16[96,666]{0,1:T(8,128)(2,1)S(1)} %copy.470, s32[5120]{0:T(1024)S(1)} %pad_clamp_fusion.1), kind=kCustom, calls=%fused_computation.30.clone | custom fusion | bytes 1787904 | tf_op jit(solution)/shard_map/jit(_take)/gather | solution.py:257
  277.7 10.1 %gather_fusion.42 = bf16[4608,96]{1,0:T(8,128)(2,1)} fusion(bf16[96,666]{0,1:T(8,128)(2,1)S(1)} %copy.470, s32[5120]{0:T(1024)S(1)} %pad_clamp_fusion.2), kind=kCustom, calls=%fused_computation.29.clone | custom fusion | bytes 1787904 | tf_op jit(solution)/shard_map/jit(_take)/gather | solution.py:257
  291.0 1.5 convolution_bitcast_fusion.6
  294.5 27.0 %all-reduce.4.cloned.1.call-done = (f32[96,2592]{0,1:T(8,128)}, f32[96,2592]{0,1:T(8,128)}) async-done(((f32[96,2592]{0,1:T(8,128)}, f32[96,2592]{0,1:T(8,128)}), (f32[96,2592]{0,1:T(8,128)}, f32[96,2592]{0,1:T(8,128)})) %all-reduce.4.cloned.1.call-update) | async-done | bytes 1990672 | tf_op jit(solution)/shard_map/psum | solution.py:348
  321.5 1.9 broadcast_multiply_fusion
  (377 shorter events, 101.3 us)
Async XLA Ops:
  7.3 314.1 %all-reduce.4.cloned.1.call-start = ((), (), s32[]{:S(2)}) async-start(), calls=%async_computation | async-start | bytes 5308416 | tf_op jit(solution)/shard_map/psum | solution.py:348
  11.3 65.2 %collective-permute-start.4 = (bf16[96,4]{1,0:T(8,128)(2,1)S(1)}, bf16[96,4]{1,0:T(8,128)(2,1)S(1)}, u32[]{:S(2)}, u32[]{:S(2)}) collective-permute-start(bf16[96,4]{1,0:T(8,128)(2,1)S(1)} %bitcast.266), channel_id=1, source_target_pairs={{12,0},{0,4},{4,8},{8,12},{13,1},{1,5},{5,9},{9,13},{14,2},{2,6},{... | collective-permute-start | bytes 2312 | tf_op jit(solution)/shard_map/ppermute | solution.py:37
  15.0 94.8 %copy-start.24 = (s32[1024]{0:T(1024)}, s32[1024]{0:T(1024)S(1)}, u32[]{:S(2)}) copy-start(s32[1024]{0:T(1024)S(1)} %pad_clamp_fusion.8) | copy-start | bytes 12292
  15.7 60.8 %collective-permute-start.3 = (bf16[96,4]{1,0:T(8,128)(2,1)S(1)}, bf16[96,4]{1,0:T(8,128)(2,1)S(1)}, u32[]{:S(2)}, u32[]{:S(2)}) collective-permute-start(bf16[96,4]{1,0:T(8,128)(2,1)S(1)} %bitcast.267), channel_id=1, source_target_pairs={{4,0},{8,4},{12,8},{0,12},{5,1},{9,5},{13,9},{1,13},{6,2},{10,6},{... | collective-permute-start | bytes 2312 | tf_op jit(solution)/shard_map/ppermute | solution.py:37
  18.4 92.0 %copy-start.25 = (s32[1024]{0:T(1024)}, s32[1024]{0:T(1024)S(1)}, u32[]{:S(2)}) copy-start(s32[1024]{0:T(1024)S(1)} %pad_clamp_fusion.10) | copy-start | bytes 12292
  19.2 57.3 %collective-permute-start.1 = (bf16[96,36]{1,0:T(8,128)(2,1)S(1)}, bf16[96,36]{1,0:T(8,128)(2,1)S(1)}, u32[]{:S(2)}, u32[]{:S(2)}) collective-permute-start(bf16[96,36]{1,0:T(8,128)(2,1)S(1)} %bitcast.272), channel_id=1, source_target_pairs={{4,0},{8,4},{12,8},{0,12},{5,1},{9,5},{13,9},{1,13},{6,2},{10,6},{... | collective-permute-start | bytes 20744 | tf_op jit(solution)/shard_map/ppermute | solution.py:37
  23.5 20.6 %collective-permute-start.9 = (s32[2,2]{0,1:T(2,128)S(1)}, s32[2,2]{0,1:T(2,128)S(1)}, u32[]{:S(2)}, u32[]{:S(2)}) collective-permute-start(s32[2,2]{0,1:T(2,128)S(1)} %bitcast.284), channel_id=1, source_target_pairs={{12,0},{0,4},{4,8},{8,12},{13,1},{1,5},{5,9},{9,13},{14,2},{2,6},{... | collective-permute-start | bytes 56 | tf_op jit(solution)/shard_map/ppermute | solution.py:37
  24.1 20.1 %collective-permute-start.8 = (s32[2,2]{0,1:T(2,128)S(1)}, s32[2,2]{0,1:T(2,128)S(1)}, u32[]{:S(2)}, u32[]{:S(2)}) collective-permute-start(s32[2,2]{0,1:T(2,128)S(1)} %bitcast.283), channel_id=1, source_target_pairs={{4,0},{8,4},{12,8},{0,12},{5,1},{9,5},{13,9},{1,13},{6,2},{10,6},{... | collective-permute-start | bytes 56 | tf_op jit(solution)/shard_map/ppermute | solution.py:37
  29.0 82.0 %copy-start.26 = (s32[1024]{0:T(1024)}, s32[1024]{0:T(1024)S(1)}, u32[]{:S(2)}) copy-start(s32[1024]{0:T(1024)S(1)} %pad_clamp_fusion.11) | copy-start | bytes 12292
  29.0 82.6 %copy-start.27 = (s32[1024]{0:T(1024)}, s32[1024]{0:T(1024)S(1)}, u32[]{:S(2)}) copy-start(s32[1024]{0:T(1024)S(1)} %pad_clamp_fusion.9) | copy-start | bytes 12292
  44.1 5.5 %collective-permute-start.5 = (s32[2,18]{0,1:T(8,128)S(1)}, s32[2,18]{0,1:T(8,128)S(1)}, u32[]{:S(2)}, u32[]{:S(2)}) collective-permute-start(s32[2,18]{0,1:T(8,128)S(1)} %bitcast.286), channel_id=1, source_target_pairs={{12,0},{0,4},{4,8},{8,12},{13,1},{1,5},{5,9},{9,13},{14,2},{2,6},{... | collective-permute-start | bytes 440 | tf_op jit(solution)/shard_map/ppermute | solution.py:37
  44.2 5.5 %collective-permute-start.6 = (s32[2,18]{0,1:T(8,128)S(1)}, s32[2,18]{0,1:T(8,128)S(1)}, u32[]{:S(2)}, u32[]{:S(2)}) collective-permute-start(s32[2,18]{0,1:T(8,128)S(1)} %bitcast.285), channel_id=1, source_target_pairs={{4,0},{8,4},{12,8},{0,12},{5,1},{9,5},{13,9},{1,13},{6,2},{10,6},{... | collective-permute-start | bytes 440 | tf_op jit(solution)/shard_map/ppermute | solution.py:37
  49.6 4.8 %collective-permute-start.7 = (s32[2,36]{0,1:T(8,128)S(1)}, s32[2,36]{0,1:T(8,128)S(1)}, u32[]{:S(2)}, u32[]{:S(2)}) collective-permute-start(s32[2,36]{0,1:T(8,128)S(1)} %bitcast.287), channel_id=1, source_target_pairs={{8,0},{12,4},{0,8},{4,12},{9,1},{13,5},{1,9},{5,13},{10,2},{14,6},... | collective-permute-start | bytes 872 | tf_op jit(solution)/shard_map/ppermute | solution.py:37
  49.7 26.8 %collective-permute-start = (bf16[96,36]{1,0:T(8,128)(2,1)S(1)}, bf16[96,36]{1,0:T(8,128)(2,1)S(1)}, u32[]{:S(2)}, u32[]{:S(2)}) collective-permute-start(bf16[96,36]{1,0:T(8,128)(2,1)S(1)} %bitcast.273), channel_id=1, source_target_pairs={{12,0},{0,4},{4,8},{8,12},{13,1},{1,5},{5,9},{9,13},{14,2},{2,6},{... | collective-permute-start | bytes 20744 | tf_op jit(solution)/shard_map/ppermute | solution.py:37
  54.4 22.1 %collective-permute-start.2 = (bf16[96,72]{1,0:T(8,128)(2,1)S(1)}, bf16[96,72]{1,0:T(8,128)(2,1)S(1)}, u32[]{:S(2)}, u32[]{:S(2)}) collective-permute-start(bf16[96,72]{1,0:T(8,128)(2,1)S(1)} %bitcast.278), channel_id=1, source_target_pairs={{8,0},{12,4},{0,8},{4,12},{9,1},{13,5},{1,9},{5,13},{10,2},{14,6},... | collective-permute-start | bytes 41480 | tf_op jit(solution)/shard_map/ppermute | solution.py:37
  76.0 31.1 %copy-start.40 = (pred[9,512]{1,0:T(8,128)(4,1)}, pred[9,512]{1,0:T(8,128)(4,1)S(1)}, u32[]{:S(2)}) copy-start(pred[9,512]{1,0:T(8,128)(4,1)S(1)} %copy.403) | copy-start | bytes 13828
  76.2 31.3 %copy-start.37 = (pred[9,512]{1,0:T(8,128)(4,1)}, pred[9,512]{1,0:T(8,128)(4,1)S(1)}, u32[]{:S(2)}) copy-start(pred[9,512]{1,0:T(8,128)(4,1)S(1)} %copy.381) | copy-start | bytes 13828
  112.9 9.2 %collective-permute-start.14 = (bf16[96,4]{1,0:T(8,128)(2,1)S(1)}, bf16[96,4]{1,0:T(8,128)(2,1)S(1)}, u32[]{:S(2)}, u32[]{:S(2)}) collective-permute-start(bf16[96,4]{1,0:T(8,128)(2,1)S(1)} %bitcast.271), channel_id=1, source_target_pairs={{12,0},{0,4},{4,8},{8,12},{13,1},{1,5},{5,9},{9,13},{14,2},{2,6},{... | collective-permute-start | bytes 2312 | tf_op jit(solution)/shard_map/ppermute | solution.py:37
  113.1 9.0 %collective-permute-start.13 = (bf16[96,4]{1,0:T(8,128)(2,1)S(1)}, bf16[96,4]{1,0:T(8,128)(2,1)S(1)}, u32[]{:S(2)}, u32[]{:S(2)}) collective-permute-start(bf16[96,4]{1,0:T(8,128)(2,1)S(1)} %bitcast.269), channel_id=1, source_target_pairs={{4,0},{8,4},{12,8},{0,12},{5,1},{9,5},{13,9},{1,13},{6,2},{10,6},{... | collective-permute-start | bytes 2312 | tf_op jit(solution)/shard_map/ppermute | solution.py:37
  116.7 5.4 %collective-permute-start.11 = (bf16[96,36]{1,0:T(8,128)(2,1)S(1)}, bf16[96,36]{1,0:T(8,128)(2,1)S(1)}, u32[]{:S(2)}, u32[]{:S(2)}) collective-permute-start(bf16[96,36]{1,0:T(8,128)(2,1)S(1)} %bitcast.277), channel_id=1, source_target_pairs={{4,0},{8,4},{12,8},{0,12},{5,1},{9,5},{13,9},{1,13},{6,2},{10,6},{... | collective-permute-start | bytes 20744 | tf_op jit(solution)/shard_map/ppermute | solution.py:37
  117.4 5.6 %collective-permute-start.10 = (bf16[96,36]{1,0:T(8,128)(2,1)S(1)}, bf16[96,36]{1,0:T(8,128)(2,1)S(1)}, u32[]{:S(2)}, u32[]{:S(2)}) collective-permute-start(bf16[96,36]{1,0:T(8,128)(2,1)S(1)} %bitcast.275), channel_id=1, source_target_pairs={{12,0},{0,4},{4,8},{8,12},{13,1},{1,5},{5,9},{9,13},{14,2},{2,6},{... | collective-permute-start | bytes 20744 | tf_op jit(solution)/shard_map/ppermute | solution.py:37
  118.8 4.8 %collective-permute-start.12 = (bf16[96,72]{1,0:T(8,128)(2,1)S(1)}, bf16[96,72]{1,0:T(8,128)(2,1)S(1)}, u32[]{:S(2)}, u32[]{:S(2)}) collective-permute-start(bf16[96,72]{1,0:T(8,128)(2,1)S(1)} %bitcast.280), channel_id=1, source_target_pairs={{8,0},{12,4},{0,8},{4,12},{9,1},{13,5},{1,9},{5,13},{10,2},{14,6},... | collective-permute-start | bytes 41480 | tf_op jit(solution)/shard_map/ppermute | solution.py:37
  170.2 9.6 %collective-permute-start.19 = (bf16[96,4]{1,0:T(8,128)(2,1)}, bf16[96,4]{1,0:T(8,128)(2,1)S(1)}, u32[]{:S(2)}, u32[]{:S(2)}) collective-permute-start(bf16[96,4]{1,0:T(8,128)(2,1)} %bitcast.59), channel_id=1, source_target_pairs={{12,0},{0,4},{4,8},{8,12},{13,1},{1,5},{5,9},{9,13},{14,2},{2,6},{... | collective-permute-start | bytes 2312 | tf_op jit(solution)/shard_map/ppermute | solution.py:37
  170.7 9.1 %collective-permute-start.18 = (bf16[96,4]{1,0:T(8,128)(2,1)}, bf16[96,4]{1,0:T(8,128)(2,1)}, u32[]{:S(2)}, u32[]{:S(2)}) collective-permute-start(bf16[96,4]{1,0:T(8,128)(2,1)} %bitcast.58), channel_id=1, source_target_pairs={{4,0},{8,4},{12,8},{0,12},{5,1},{9,5},{13,9},{1,13},{6,2},{10,6},{... | collective-permute-start | bytes 2312 | tf_op jit(solution)/shard_map/ppermute | solution.py:37
  174.0 5.7 %collective-permute-start.16 = (bf16[96,36]{1,0:T(8,128)(2,1)}, bf16[96,36]{1,0:T(8,128)(2,1)}, u32[]{:S(2)}, u32[]{:S(2)}) collective-permute-start(bf16[96,36]{1,0:T(8,128)(2,1)} %bitcast.56), channel_id=1, source_target_pairs={{4,0},{8,4},{12,8},{0,12},{5,1},{9,5},{13,9},{1,13},{6,2},{10,6},{... | collective-permute-start | bytes 20744 | tf_op jit(solution)/shard_map/ppermute | solution.py:37
  174.7 5.9 %collective-permute-start.15 = (bf16[96,36]{1,0:T(8,128)(2,1)}, bf16[96,36]{1,0:T(8,128)(2,1)}, u32[]{:S(2)}, u32[]{:S(2)}) collective-permute-start(bf16[96,36]{1,0:T(8,128)(2,1)} %bitcast.55), channel_id=1, source_target_pairs={{12,0},{0,4},{4,8},{8,12},{13,1},{1,5},{5,9},{9,13},{14,2},{2,6},{... | collective-permute-start | bytes 20744 | tf_op jit(solution)/shard_map/ppermute | solution.py:37
  176.1 5.0 %collective-permute-start.17 = (bf16[96,72]{1,0:T(8,128)(2,1)}, bf16[96,72]{1,0:T(8,128)(2,1)}, u32[]{:S(2)}, u32[]{:S(2)}) collective-permute-start(bf16[96,72]{1,0:T(8,128)(2,1)} %bitcast.57), channel_id=1, source_target_pairs={{8,0},{12,4},{0,8},{4,12},{9,1},{13,5},{1,9},{5,13},{10,2},{14,6},... | collective-permute-start | bytes 41480 | tf_op jit(solution)/shard_map/ppermute | solution.py:37
  223.3 36.5 %collective-permute-start.24 = (bf16[96,4]{1,0:T(8,128)(2,1)S(1)}, bf16[96,4]{1,0:T(8,128)(2,1)S(1)}, u32[]{:S(2)}, u32[]{:S(2)}) collective-permute-start(bf16[96,4]{1,0:T(8,128)(2,1)S(1)} %bitcast.270), channel_id=1, source_target_pairs={{12,0},{0,4},{4,8},{8,12},{13,1},{1,5},{5,9},{9,13},{14,2},{2,6},{... | collective-permute-start | bytes 2312 | tf_op jit(solution)/shard_map/ppermute | solution.py:37
  225.0 34.8 %collective-permute-start.23 = (bf16[96,4]{1,0:T(8,128)(2,1)S(1)}, bf16[96,4]{1,0:T(8,128)(2,1)S(1)}, u32[]{:S(2)}, u32[]{:S(2)}) collective-permute-start(bf16[96,4]{1,0:T(8,128)(2,1)S(1)} %bitcast.268), channel_id=1, source_target_pairs={{4,0},{8,4},{12,8},{0,12},{5,1},{9,5},{13,9},{1,13},{6,2},{10,6},{... | collective-permute-start | bytes 2312 | tf_op jit(solution)/shard_map/ppermute | solution.py:37
  227.2 32.6 %collective-permute-start.21 = (bf16[96,36]{1,0:T(8,128)(2,1)S(1)}, bf16[96,36]{1,0:T(8,128)(2,1)S(1)}, u32[]{:S(2)}, u32[]{:S(2)}) collective-permute-start(bf16[96,36]{1,0:T(8,128)(2,1)S(1)} %bitcast.276), channel_id=1, source_target_pairs={{4,0},{8,4},{12,8},{0,12},{5,1},{9,5},{13,9},{1,13},{6,2},{10,6},{... | collective-permute-start | bytes 20744 | tf_op jit(solution)/shard_map/ppermute | solution.py:37
  227.8 32.0 %collective-permute-start.20 = (bf16[96,36]{1,0:T(8,128)(2,1)S(1)}, bf16[96,36]{1,0:T(8,128)(2,1)S(1)}, u32[]{:S(2)}, u32[]{:S(2)}) collective-permute-start(bf16[96,36]{1,0:T(8,128)(2,1)S(1)} %bitcast.274), channel_id=1, source_target_pairs={{12,0},{0,4},{4,8},{8,12},{13,1},{1,5},{5,9},{9,13},{14,2},{2,6},{... | collective-permute-start | bytes 20744 | tf_op jit(solution)/shard_map/ppermute | solution.py:37
  229.2 30.6 %collective-permute-start.22 = (bf16[96,72]{1,0:T(8,128)(2,1)S(1)}, bf16[96,72]{1,0:T(8,128)(2,1)S(1)}, u32[]{:S(2)}, u32[]{:S(2)}) collective-permute-start(bf16[96,72]{1,0:T(8,128)(2,1)S(1)} %bitcast.279), channel_id=1, source_target_pairs={{8,0},{12,4},{0,8},{4,12},{9,1},{13,5},{1,9},{5,13},{10,2},{14,6},... | collective-permute-start | bytes 41480 | tf_op jit(solution)/shard_map/ppermute | solution.py:37
  (59 other events, 446.3 us)
Sparse Core Ops, SparseCore 0:
  219.2 102.1 all-reduce.3
where the time goes:
time: 334 us; the launch traced here: 333 us
  local copies, waits for them, and re-layouts  193 us (58%)
  waiting for transfers between devices  35.4 us (11%)
  starting transfers between devices  34.3 us (10%)
  blocking collectives  30 us (9%)
  between operations  15.5 us (5%)
  matrix products  15 us (4%)
  other arithmetic  9.9 us (3%)
    gather x12, local copies, waits for them, and re-layouts, convolve(): jnp.take(source_table, gather_index[9 * group_number:9 * group_number + 9...  59.9 us
    gather x12, local copies, waits for them, and re-layouts, convolve_back(): jnp.take(source_table, flipped[9 * group_number:9 * group_number + 9], ax...  59.1 us
    ppermute x25, starting transfers between devices, shifted(): return lax.ppermute(block, axis, route)  34.2 us
    psum x1, blocking collectives, on_device(): lax.psum((weight_one_part, bias_one_part, weight_two_part, bias_two_part)...  30 us
    psum x1, waiting for transfers between devices, on_device(): lax.psum((weight_one_part, bias_one_part, weight_two_part, bias_two_part)...  27 us
    gather x40, local copies, waits for them, and re-layouts, move_rows(): arrived.append(mover(jnp.take(own_rows, row_index, axis=1), offset))  18.2 us
    unnamed x140, local copies, waits for them, and re-layouts  15.6 us
    ppermute x25, waiting for transfers between devices, shifted(): return lax.ppermute(block, axis, route)  8.44 us
  transfers between devices with their start and end apart: 26, of which 7 were waited for; matrix products, arithmetic and copies ran while one was open for 26% of the time, Pallas kernels for 0%

commit v1 on v0

v1 whole, which is shorter than its diff:
```python
import functools

import jax
import jax.numpy as jnp
import numpy as np
from jax import lax
from jax.experimental import pallas as pl
from jax.experimental.pallas import tpu as pltpu
from jax.sharding import PartitionSpec as P

C = 96
LANES = 128
SIDE = 8
KMAX = 2
LOW = 2
LEVELS = 4
EDGE = 2 * SIDE
PLANE = EDGE * EDGE
CELLS = LEVELS * PLANE
WIDE = EDGE * (EDGE + 2)
ROWS = 4 * SIDE * SIDE * KMAX
TAPS = 27
DEPTH = TAPS * LANES
BF16 = jnp.bfloat16
F32 = jnp.float32
MESH = pl.DeviceIdType.MESH


def side_offsets(parties):
    half = parties // 2
    found = []
    for offset in (1, parties - 1, (half + 1) % parties, (half - 1) % parties):
        if offset not in found:
            found.append(offset)
    return found


def dot(left, right, dims=((1,), (0,))):
    return lax.dot_general(left, right, (dims, ((), ())), preferred_element_type=F32)


def slope_of(values):
    squash = jax.nn.sigmoid(values)
    return squash * (1.0 + values * (1.0 - squash))


def iota(shape, axis):
    return lax.broadcasted_iota(jnp.int32, shape, axis)


def one_hot(condition):
    return jnp.where(condition, 1.0, 0.0).astype(BF16)


def kernel(
    parties,
    features,
    grad_out,
    target,
    flags,
    weight_one,
    weight_two,
    bias_one,
    bias_two,
    out_features,
    input_grad,
    grad_w_one,
    grad_w_two,
    grad_b_one,
    grad_b_two,
    place,
    spread_left,
    spread_right,
    pick,
    turned,
    back,
    taps_one,
    taps_two,
    taps_back,
    pre_kept,
    mask_kept,
    send_side,
    send_across,
    got_side,
    got_across,
    send_sem,
    recv_sem,
):
    offsets = side_offsets(parties)
    half = parties // 2
    me = lax.axis_index("blocks")
    partners = offsets + [half]

    barrier = pltpu.get_barrier_semaphore()
    for offset in partners:
        pl.semaphore_signal(
            barrier, inc=1, device_id={"blocks": lax.rem(me + offset, parties)}, device_id_type=MESH
        )

    place[...] = one_hot(iota((CELLS, ROWS), 0) == target[...])
    mask_kept[...] = dot(place[...], jnp.ones((ROWS, LANES), BF16))

    row = iota((LEVELS * WIDE, LANES), 0)
    level = row // WIDE
    across = (row % WIDE) // EDGE
    along = row % EDGE
    wanted = jnp.where(
        across == 0,
        64 + level * EDGE + EDGE - 1,
        jnp.where(across == EDGE + 1, 64 + level * EDGE, level * EDGE + across - 1),
    )
    lane = iota((LEVELS * WIDE, LANES), 1)
    spread_left[...] = one_hot((along == 0) & (lane == wanted))
    spread_right[...] = one_hot((along == EDGE - 1) & (lane == wanted))
    number = iota((128, CELLS), 0)
    spot = (number % 64) * EDGE + jnp.where(number >= 64, EDGE - 1, 0)
    pick[...] = one_hot(iota((128, CELLS), 1) == spot)

    for taps in (taps_one, taps_two, taps_back):
        taps[0] = jnp.zeros((WIDE, 3 * LANES), BF16)
        taps[LEVELS + 1] = jnp.zeros((WIDE, 3 * LANES), BF16)

    def dense(rows_ref):
        padded = jnp.concatenate([rows_ref[...], jnp.zeros((LANES - C, ROWS), BF16)], axis=0)
        return dot(place[...], padded, ((1,), (1,))).astype(BF16)

    def sparse(cells):
        return dot(jnp.transpose(cells), place[...])[:C].astype(BF16)

    def copies(turn):
        result = []
        for slot, offset in enumerate(offsets):
            result.append(
                pltpu.make_async_remote_copy(
                    src_ref=send_side.at[turn],
                    dst_ref=got_side.at[turn, slot],
                    send_sem=send_sem.at[turn, slot],
                    recv_sem=recv_sem.at[turn, slot],
                    device_id={"blocks": lax.rem(me + offset, parties)},
                    device_id_type=MESH,
                )
            )
        result.append(
            pltpu.make_async_remote_copy(
                src_ref=send_across.at[turn],
                dst_ref=got_across.at[turn],
                send_sem=send_sem.at[turn, len(offsets)],
                recv_sem=recv_sem.at[turn, len(offsets)],
                device_id={"blocks": lax.rem(me + half, parties)},
                device_id_type=MESH,
            )
        )
        return result

    def send(turn, cells):
        send_side[turn] = dot(pick[...], cells).astype(BF16)
        for z in range(LEVELS):
            send_across[turn, z * EDGE : (z + 1) * EDGE] = cells[z * PLANE : z * PLANE + EDGE]
            send_across[turn, 64 + z * EDGE : 64 + (z + 1) * EDGE] = cells[
                (z + 1) * PLANE - EDGE : (z + 1) * PLANE
            ]
        for copy in copies(turn):
            copy.start()

    up = flags[0:1] > 0
    down = flags[1:2] > 0
    left = flags[2:3] > 0
    right = flags[3:4] > 0

    def arrive(turn, cells, taps):
        for copy in copies(turn):
            copy.wait()
        inside = iota((64, LANES), 0) % EDGE
        corner = ((inside == EDGE - 1) & up) | ((inside == 0) & down)

        def columns(main, diagonal, first, there):
            straight = got_side[turn, offsets.index(main), first : first + 64]
            slanted = got_side[turn, offsets.index(diagonal), first : first + 64]
            both = jnp.concatenate(
                [
                    jnp.where(there, straight.astype(F32), 0.0),
                    jnp.where(corner & there, slanted.astype(F32), 0.0),
                ],
                axis=0,
            )
            return both.astype(BF16)

        from_left = columns(1, (half + 1) % parties, 64, left)
        from_right = columns(parties - 1, (half - 1) % parties, 0, right)
        pieces = []
        for z in range(LEVELS):
            above = got_across[turn, 64 + z * EDGE : 64 + (z + 1) * EDGE].astype(F32)
            below = got_across[turn, z * EDGE : (z + 1) * EDGE].astype(F32)
            pieces.append(jnp.where(up, above, 0.0))
            pieces.append(cells[z * PLANE : (z + 1) * PLANE].astype(F32))
            pieces.append(jnp.where(down, below, 0.0))
        middle = jnp.concatenate(pieces, axis=0)
        place_along = iota((LEVELS * WIDE, LANES), 0) % EDGE
        before = jnp.where(place_along == 0, 0.0, pltpu.roll(middle, 1, 0))
        after = jnp.where(place_along == EDGE - 1, 0.0, pltpu.roll(middle, LEVELS * WIDE - 1, 0))
        before = (before + dot(spread_left[...], from_left)).astype(BF16)
        after = (after + dot(spread_right[...], from_right)).astype(BF16)
        middle = middle.astype(BF16)
        for z in range(LEVELS):
            part = slice(z * WIDE, (z + 1) * WIDE)
            taps[z + 1, :, 0:LANES] = before[part]
            taps[z + 1, :, LANES : 2 * LANES] = middle[part]
            taps[z + 1, :, 2 * LANES : 3 * LANES] = after[part]

    def convolve(taps, weights):
        results = []
        for z in range(LEVELS):
            parts = [
                taps[z + dz, dx * EDGE : dx * EDGE + PLANE] for dz in range(3) for dx in range(3)
            ]
            results.append(dot(jnp.concatenate(parts, axis=1), weights))
        return jnp.concatenate(results, axis=0)

    def weight_grad(gradient, taps, out):
        flipped = jnp.transpose(gradient)[:C]
        for dz in range(3):
            for dx in range(3):
                field = jnp.concatenate(
                    [taps[z + dz, dx * EDGE : dx * EDGE + PLANE] for z in range(LEVELS)], axis=0
                )
                first = (3 * dz + dx) * 3 * LANES
                out[:, first : first + 3 * LANES] = dot(flipped, field)

    def turn_back(weights):
        for tap in range(TAPS):
            other = TAPS - 1 - tap
            back[tap * LANES : (tap + 1) * LANES] = weights[
                :, other * LANES : (other + 1) * LANES
            ]

    live = mask_kept[...] > 0
    cells = dense(features)
    pl.semaphore_wait(barrier, len(partners))
    send(0, cells)
    turned[...] = jnp.transpose(weight_one[...])
    arrive(0, cells, taps_one)

    pre_one = convolve(taps_one, turned[...]) + bias_one[...]
    pre_kept[...] = pre_one
    hidden = jnp.where(live, pre_one * jax.nn.sigmoid(pre_one), 0.0).astype(BF16)
    send(1, hidden)
    turned[...] = jnp.transpose(weight_two[...])
    upstream = dense(grad_out)
    turn_back(weight_two)
    arrive(1, hidden, taps_two)

    pre_two = convolve(taps_two, turned[...]) + bias_two[...]
    grad_two = jnp.where(live, upstream.astype(F32) * slope_of(pre_two), 0.0).astype(BF16)
    send(2, grad_two)
    activated = jnp.where(live, pre_two * jax.nn.sigmoid(pre_two), 0.0).astype(BF16)
    out_features[...] = sparse(activated)
    weight_grad(grad_two, taps_two, grad_w_two)
    grad_b_two[...] = jnp.sum(grad_two.astype(F32), axis=0, keepdims=True)
    arrive(2, grad_two, taps_back)

    hidden_sum = convolve(taps_back, back[...])
    grad_one = jnp.where(live, hidden_sum * slope_of(pre_kept[...]), 0.0).astype(BF16)
    send(3, grad_one)
    turn_back(weight_one)
    weight_grad(grad_one, taps_one, grad_w_one)
    grad_b_one[...] = jnp.sum(grad_one.astype(F32), axis=0, keepdims=True)
    arrive(3, grad_one, taps_back)
    input_grad[...] = sparse(convolve(taps_back, back[...]).astype(BF16))


def tap_major(weights):
    kernel_taps = weights.reshape(C, C, TAPS).transpose(0, 2, 1)
    padded = jnp.pad(kernel_taps, ((0, LANES - C), (0, 0), (0, LANES - C)))
    return padded.reshape(LANES, DEPTH)


def channel_major(gradient):
    return gradient.reshape(C, TAPS, LANES)[:, :, :C].transpose(0, 2, 1).reshape(C, C * TAPS)


def on_device(
    features, grad_out, weight_one, weight_two, bias_one, bias_two, heights, counts, neighbours
):
    parties = lax.axis_size("blocks")
    sides = len(side_offsets(parties))
    block = np.arange(4)[:, None]
    column = np.arange(SIDE * SIDE)[None, :]
    cell = (SIDE * (block // 2) + column // SIDE) * EDGE + SIDE * (block % 2) + column % SIDE
    layer = np.arange(KMAX)[None, None, :]
    target = jnp.where(
        layer < counts[0][:, :, None],
        (heights[0][:, :, None] - LOW + layer) * PLANE + cell[:, :, None],
        -1,
    )
    target = target.astype(jnp.int32).reshape(1, ROWS)
    near = neighbours[0]
    flags = jnp.stack([near[0, 1], near[2, 0], near[0, 3], near[1, 2]]) >= 0
    flags = jnp.broadcast_to(jnp.pad(flags.astype(jnp.int32), (0, 4))[:, None], (8, LANES))
    bias = [jnp.pad(value, (0, LANES - C))[None] for value in (bias_one, bias_two)]
    vmem = pl.BlockSpec(memory_space=pltpu.VMEM)
    results = pl.pallas_call(
        functools.partial(kernel, parties),
        out_shape=(
            jax.ShapeDtypeStruct((C, ROWS), BF16),
            jax.ShapeDtypeStruct((C, ROWS), BF16),
            jax.ShapeDtypeStruct((C, DEPTH), F32),
            jax.ShapeDtypeStruct((C, DEPTH), F32),
            jax.ShapeDtypeStruct((1, LANES), F32),
            jax.ShapeDtypeStruct((1, LANES), F32),
        ),
        in_specs=[vmem] * 8,
        out_specs=[vmem] * 6,
        scratch_shapes=[
            pltpu.VMEM((CELLS, ROWS), BF16),
            pltpu.VMEM((LEVELS * WIDE, LANES), BF16),
            pltpu.VMEM((LEVELS * WIDE, LANES), BF16),
            pltpu.VMEM((128, CELLS), BF16),
            pltpu.VMEM((DEPTH, LANES), BF16),
            pltpu.VMEM((DEPTH, LANES), BF16),
            pltpu.VMEM((LEVELS + 2, WIDE, 3 * LANES), BF16),
            pltpu.VMEM((LEVELS + 2, WIDE, 3 * LANES), BF16),
            pltpu.VMEM((LEVELS + 2, WIDE, 3 * LANES), BF16),
            pltpu.VMEM((CELLS, LANES), F32),
            pltpu.VMEM((CELLS, LANES), F32),
            pltpu.VMEM((4, 128, LANES), BF16),
            pltpu.VMEM((4, 128, LANES), BF16),
            pltpu.VMEM((4, sides, 128, LANES), BF16),
            pltpu.VMEM((4, 128, LANES), BF16),
            pltpu.SemaphoreType.DMA((4, sides + 1)),
            pltpu.SemaphoreType.DMA((4, sides + 1)),
        ],
        compiler_params=pltpu.CompilerParams(
            collective_id=0, has_side_effects=True, vmem_limit_bytes=48 * 1024 * 1024
        ),
    )(
        features[0],
        grad_out[0],
        target,
        flags,
        tap_major(weight_one),
        tap_major(weight_two),
        bias[0],
        bias[1],
    )
    shards = parties * lax.axis_size("dp") * lax.axis_size("sub")
    summed = lax.psum(results[2:], ("blocks", "dp", "sub"))
    scale = 1.0 / shards
    return (
        results[0][None],
        results[1][None],
        channel_major(summed[0]) * scale,
        channel_major(summed[1]) * scale,
        summed[2][0, :C] * scale,
        summed[3][0, :C] * scale,
    )


def solution(mesh):
    placed = (
        P(("groups", "dp", "sub"), None, "blocks"),
        P(("groups", "dp", "sub"), None, "blocks"),
        P(),
        P(),
        P(),
        P(),
        P(("groups", "dp", "sub"), "blocks", None),
        P(("groups", "dp", "sub"), "blocks", None),
        P(("groups", "dp", "sub"), "blocks", None),
    )
    return jax.shard_map(
        on_device,
        mesh=mesh,
        in_specs=placed,
        out_specs=(
            P(("groups", "dp", "sub"), None, "blocks"),
            P(("groups", "dp", "sub"), None, "blocks"),
            P("groups", None),
            P("groups", None),
            P("groups"),
            P("groups"),
        ),
        check_vma=False,
    )
```

time: 334 us -> 175 us (0.52)
  local copies, waits for them, and re-layouts: 193 us -> 19.5 us
  waiting for transfers between devices: 35.4 us -> 72 us
  starting transfers between devices: 34.3 us -> 0.04 us
  Pallas kernels: 0 us -> 32.2 us
  matrix products: 15 us -> 0 us
    gather x83 -> x0, local copies, waits for them, and re-layouts: 158 us -> none  [the longest x12 59.9 us: convolve(): jnp.take(source_table, gather_index[9 * group_number:9 * group_number + 9...]
    psum x1, waiting for transfers between devices: 27 us -> 72 us  [on_device(): summed = lax.psum(results[2:], ('blocks', 'dp', 'sub'))]
    ppermute x25 -> x0, starting transfers between devices: 34.2 us -> none  [shifted(): return lax.ppermute(block, axis, route)]
    pallas_call x0 -> x1, Pallas kernels: none -> 32.2 us  [on_device(): pl.pallas_call(functools.partial(kernel, parties), out_shape=(jax.ShapeDt...]
    dot_general x18 -> x0, matrix products: 15 us -> none  [the longest x6 5.07 us: convolve(): jnp.einsum('oik,ikr->or', kernel[:, :, 9 * group_number:9 * group_number...]
    ppermute x25 -> x0, waiting for transfers between devices: 8.44 us -> none  [shifted(): return lax.ppermute(block, axis, route)]
    unnamed x140 -> x22, local copies, waits for them, and re-layouts: 15.6 us -> 7.44 us
    concatenate x11 -> x0, local copies, waits for them, and re-layouts: 4.75 us -> none  [the longest x2 2.75 us: kernel_grad(): return jnp.concatenate(pieces, axis=2).reshape(C, C * 27)]
  transfers between devices with their start and end apart: 26 -> 1, of which waited for: 7 -> 1; matrix products, arithmetic and copies ran while one was open for 26% -> 1% of each run, Pallas kernels for 0% -> 0%
where the time goes in v1:
time: 175 us
  waiting for transfers between devices  72 us (41%)
  Pallas kernels  32.2 us (18%)
  blocking collectives  30.1 us (17%)
  local copies, waits for them, and re-layouts  19.5 us (11%)
  between operations  14.3 us (8%)
  other arithmetic  6.97 us (4%)
    psum x1, waiting for transfers between devices, on_device(): summed = lax.psum(results[2:], ('blocks', 'dp', 'sub'))  72 us
    pallas_call x1, Pallas kernels, on_device(): pl.pallas_call(functools.partial(kernel, parties), out_shape=(jax.ShapeDt...  32.2 us
    psum x1, blocking collectives, on_device(): summed = lax.psum(results[2:], ('blocks', 'dp', 'sub'))  30.1 us
    unnamed x22, local copies, waits for them, and re-layouts  7.44 us
    reshape x2, local copies, waits for them, and re-layouts, channel_major(): gradient.reshape(C, TAPS, LANES)[:, :, :C].transpose(0, 2, 1)  3.99 us
  transfers between devices with their start and end apart: 1, of which 1 were waited for; matrix products, arithmetic and copies ran while one was open for 1% of the time, Pallas kernels for 0%

profile of v1, /device:TPU:0, one launch (start us, length us, event | category | flops | bytes accessed | tf_op | source)
XLA Modules:
  0.0 175.1 jit_solution(17584363836288191441)
XLA Ops:
  7.2 0.7 add_bitcast_fusion
  7.9 1.4 fusion.5
  9.3 2.7 %add_compare_fusion = pred[4]{0:T(512)(128)(4,1)S(1)} fusion(s32[1]{0:T(128)} %bitcast.8, s32[1]{0:T(128)} %bitcast.7, s32[1]{0:T(128)} %bitcast.6, s32[1]{0:T(128)} %bitcast.5), kind=kLoop, calls=%fused_computation.11 | loop fusion | flops 16 | bytes 20 | tf_op jit(solution)/shard_map/ge | solution.py:297
  12.0 0.9 fusion.4
  12.9 0.1 select_n.15.target
  13.0 1.4 copy.21
  14.4 0.2 reshape.119
  14.6 0.3 copy.31
  14.9 0.2 pad.23.clone
  15.1 1.0 copy.25.weight_one
  16.1 0.3 copy.23
  16.4 0.2 reshape.121
  16.6 0.3 copy.32
  17.0 0.2 pad.24.clone
  17.2 1.2 copy.26.weight_two
  18.5 32.2 %shard_map.154 = (bf16[96,512]{1,0:T(8,128)(2,1)S(1)}, bf16[96,512]{1,0:T(8,128)(2,1)S(1)}, f32[96,3456]{1,0:T(8,128)S(1)}, f32[96,3456]{1,0:T(8,128)S(1)}, f32[1,128]{1,0:T(1,128)S(1)}, /*index=5*/f32[1,128]{1,0:T(1,128)S(1)}) custom-call(bf16[96,512]{1,0:T(8,128)(2,1)S(1)} %bitcast.36, bf16[96,512]{1,0:T(8,128)(2,1)S(1)} %bitcast.37, ...), custom_call_target="tpu_custom_call" | custom-call | tf_op jit(solution)/shard_map/pallas_call | solution.py:301
  50.7 1.1 copy-done
  51.8 2.6 %reshape.123 = f32[96,27,128]{2,1,0:T(8,128)} reshape(f32[96,3456]{1,0:T(8,128)} %copy-done) | data formatting | bytes 2654208 | tf_op jit(solution)/shard_map/reshape | solution.py:278
  54.3 1.4 reshape.124
  55.8 30.1 %all-reduce.5 = (f32[1,128]{1,0:T(1,128)S(1)}, f32[1,128]{1,0:T(1,128)S(1)}) all-reduce(f32[1,128]{1,0:T(1,128)S(1)} %get-tuple-element.16, f32[1,128]{1,0:T(1,128)S(1)} %get-tuple-element.17), channel_id=1, replica_groups=mesh['groups'=2,'blocks'=4,'dp'=2,'sub'=2] {'blocks','dp','sub'}, use_global_device_ids=true, to_apply=%region_2.3 | all-reduce | flops 256 | bytes 2048 | tf_op jit(solution)/shard_map/psum | solution.py:346
  85.9 0.5 multiply_bitcast_fusion.1
  86.5 0.5 multiply_bitcast_fusion
  87.0 72.0 %all-reduce.9.cloned.1.call-done = (f32[96,27,128]{2,1,0:T(8,128)}, f32[96,27,128]{2,1,0:T(8,128)}) async-done(((f32[96,27,128]{2,1,0:T(8,128)}, f32[96,27,128]{2,1,0:T(8,128)}), (f32[96,27,128]{2,1,0:T(8,128)}, f32[96,27,128]{2,1,0:T(8,128)})) %all-reduce.9.cloned.1.call-update) | async-done | bytes 2654224 | tf_op jit(solution)/shard_map/psum | solution.py:346
  158.9 1.6 fusion.1
  160.5 1.6 copy.27
  162.2 1.4 copy.29
  163.7 0.2 fusion
  163.9 1.6 copy.28
  165.5 0.1 mul.51
  165.6 1.4 copy.30
  167.0 0.6 copy.37
  167.6 0.6 copy.38
  (19 shorter events, 0.3 us)
Async XLA Ops:
  7.2 151.8 %all-reduce.9.cloned.1.call-start = ((), (), s32[]{:S(2)}) async-start(), calls=%async_computation | async-start | bytes 6291456 | tf_op jit(solution)/shard_map/psum | solution.py:346
  14.9 1.3 copy-start.4
  16.9 1.5 copy-start.5
  16.9 1.5 copy-start.6
  16.9 1.6 copy-start.1
  17.0 1.5 copy-start.2
  50.7 1.1 copy-start
  162.2 1.5 copy-start.3
Sparse Core Ops, SparseCore 0:
  55.9 102.9 all-reduce.8

commit v2 on v1

--- a/solution.py
+++ b/solution.py
@@ -21,6 +21,8 @@
 ROWS = 4 * SIDE * SIDE * KMAX
 TAPS = 27
 DEPTH = TAPS * LANES
+TILES = 21
+SUM_ROWS = 2048
 BF16 = jnp.bfloat16
 F32 = jnp.float32
 MESH = pl.DeviceIdType.MESH
@@ -64,10 +66,8 @@
     bias_two,
     out_features,
     input_grad,
-    grad_w_one,
-    grad_w_two,
-    grad_b_one,
-    grad_b_two,
+    sum_one,
+    sum_two,
     place,
     spread_left,
     spread_right,
@@ -83,19 +83,34 @@
     send_across,
     got_side,
     got_across,
+    packed,
+    part,
+    part_sent,
+    got_core,
+    core_sum,
+    core_sent,
+    got_chip,
+    chip_sum,
+    chip_sent,
+    got_line,
+    total,
     send_sem,
     recv_sem,
+    sum_send,
+    sum_recv,
 ):
     offsets = side_offsets(parties)
     half = parties // 2
     me = lax.axis_index("blocks")
-    partners = offsets + [half]
+    chip = lax.axis_index("dp")
+    core = lax.axis_index("sub")
+    share = SUM_ROWS // 4 // parties
+    partners = [{"blocks": lax.rem(me + offset, parties)} for offset in range(1, parties)]
+    partners += [{"dp": 1 - chip}, {"sub": 1 - core}]
 
     barrier = pltpu.get_barrier_semaphore()
-    for offset in partners:
-        pl.semaphore_signal(
-            barrier, inc=1, device_id={"blocks": lax.rem(me + offset, parties)}, device_id_type=MESH
-        )
+    for partner in partners:
+        pl.semaphore_signal(barrier, inc=1, device_id=partner, device_id_type=MESH)
 
     place[...] = one_hot(iota((CELLS, ROWS), 0) == target[...])
     mask_kept[...] = dot(place[...], jnp.ones((ROWS, LANES), BF16))
@@ -119,6 +134,11 @@
     for taps in (taps_one, taps_two, taps_back):
         taps[0] = jnp.zeros((WIDE, 3 * LANES), BF16)
         taps[LEVELS + 1] = jnp.zeros((WIDE, 3 * LANES), BF16)
+
+    for layer in range(2):
+        spare = SUM_ROWS - TILES * C
+        part[layer, TILES * C :] = jnp.zeros((spare, LANES), F32)
+        part_sent[layer, TILES * C :] = jnp.zeros((spare, LANES), BF16)
 
     def dense(rows_ref):
         padded = jnp.concatenate([rows_ref[...], jnp.zeros((LANES - C, ROWS), BF16)], axis=0)
@@ -216,15 +236,112 @@
             results.append(dot(jnp.concatenate(parts, axis=1), weights))
         return jnp.concatenate(results, axis=0)
 
-    def weight_grad(gradient, taps, out):
+    def weight_grad(gradient, taps, layer):
         flipped = jnp.transpose(gradient)[:C]
         for dz in range(3):
             for dx in range(3):
                 field = jnp.concatenate(
                     [taps[z + dz, dx * EDGE : dx * EDGE + PLANE] for z in range(LEVELS)], axis=0
                 )
-                first = (3 * dz + dx) * 3 * LANES
-                out[:, first : first + 3 * LANES] = dot(flipped, field)
+                product = dot(flipped, field)
+                for dy in range(3):
+                    first = ((3 * dz + dx) * 3 + dy) * C
+                    packed[:, first : first + C] = product[:, dy * LANES : dy * LANES + C]
+        bias = dot(flipped, jnp.ones((CELLS, LANES), BF16))
+        packed[:, TAPS * C : (TAPS + 1) * C] = bias[:, :C]
+        for tile in range(TILES):
+            piece = packed[:, tile * LANES : (tile + 1) * LANES]
+            part[layer, tile * C : (tile + 1) * C] = piece
+            part_sent[layer, tile * C : (tile + 1) * C] = piece.astype(BF16)
+
+    half_rows, quarter = SUM_ROWS // 2, SUM_ROWS // 4
+    mine = core * half_rows + chip * quarter
+
+    def remote(source, landing, layer, number, partner):
+        return pltpu.make_async_remote_copy(
+            src_ref=source,
+            dst_ref=landing,
+            send_sem=sum_send.at[layer, number],
+            recv_sem=sum_recv.at[layer, number],
+            device_id=partner,
+            device_id_type=MESH,
+        )
+
+    def over_cores(layer):
+        other = pl.ds(pl.multiple_of((1 - core) * half_rows, 16), half_rows)
+        return [
+            remote(part_sent.at[layer, other], got_core.at[layer], layer, 0, {"sub": 1 - core})
+        ]
+
+    def over_chips(layer):
+        other = pl.ds(pl.multiple_of((1 - chip) * quarter, 16), quarter)
+        return [
+            remote(core_sent.at[layer, other], got_chip.at[layer], layer, 1, {"dp": 1 - chip})
+        ]
+
+    def over_line(layer):
+        result = []
+        for offset in range(1, parties):
+            there = lax.rem(me + offset, parties)
+            rows = pl.ds(pl.multiple_of(there * share, 16), share)
+            result.append(
+                remote(
+                    chip_sent.at[layer, rows],
+                    got_line.at[layer, offset - 1],
+                    layer,
+                    1 + offset,
+                    {"blocks": there},
+                )
+            )
+        return result
+
+    def spread_line(layer):
+        rows = total.at[layer, pl.ds(pl.multiple_of(mine + me * share, 16), share)]
+        return [
+            remote(rows, rows, layer, parties + offset, {"blocks": lax.rem(me + offset, parties)})
+            for offset in range(1, parties)
+        ]
+
+    def spread_chips(layer):
+        rows = total.at[layer, pl.ds(pl.multiple_of(mine, 16), quarter)]
+        return [remote(rows, rows, layer, 2 * parties, {"dp": 1 - chip})]
+
+    def spread_cores(layer):
+        rows = total.at[layer, pl.ds(pl.multiple_of(core * half_rows, 16), half_rows)]
+        return [remote(rows, rows, layer, 2 * parties + 1, {"sub": 1 - core})]
+
+    def begin(copies_of, layer):
+        for copy in copies_of(layer):
+            copy.start()
+
+    def finish(copies_of, layer):
+        for copy in copies_of(layer):
+            copy.wait()
+
+    def sum_cores(layer):
+        finish(over_cores, layer)
+        own = part[layer, pl.ds(pl.multiple_of(core * half_rows, 16), half_rows)]
+        value = own + got_core[layer].astype(F32)
+        core_sum[layer] = value
+        core_sent[layer] = value.astype(BF16)
+        begin(over_chips, layer)
+
+    def sum_chips(layer):
+        finish(over_chips, layer)
+        own = core_sum[layer, pl.ds(pl.multiple_of(chip * quarter, 16), quarter)]
+        value = own + got_chip[layer].astype(F32)
+        chip_sum[layer] = value
+        chip_sent[layer] = value.astype(BF16)
+        begin(over_line, layer)
+
+    def sum_line(layer):
+        finish(over_line, layer)
+        value = chip_sum[layer, pl.ds(pl.multiple_of(me * share, 16), share)]
+        for offset in range(1, parties):
+            value = value + got_line[layer, offset - 1].astype(F32)
+        value = value * (1.0 / (4 * parties))
+        total[layer, pl.ds(pl.multiple_of(mine + me * share, 16), share)] = value.astype(BF16)
+        begin(spread_line, layer)
 
     def turn_back(weights):
         for tap in range(TAPS):
@@ -254,18 +371,37 @@
     send(2, grad_two)
     activated = jnp.where(live, pre_two * jax.nn.sigmoid(pre_two), 0.0).astype(BF16)
     out_features[...] = sparse(activated)
-    weight_grad(grad_two, taps_two, grad_w_two)
-    grad_b_two[...] = jnp.sum(grad_two.astype(F32), axis=0, keepdims=True)
+    weight_grad(grad_two, taps_two, 0)
+    begin(over_cores, 0)
     arrive(2, grad_two, taps_back)
+    sum_cores(0)
 
     hidden_sum = convolve(taps_back, back[...])
     grad_one = jnp.where(live, hidden_sum * slope_of(pre_kept[...]), 0.0).astype(BF16)
     send(3, grad_one)
+    sum_chips(0)
     turn_back(weight_one)
-    weight_grad(grad_one, taps_one, grad_w_one)
-    grad_b_one[...] = jnp.sum(grad_one.astype(F32), axis=0, keepdims=True)
+    weight_grad(grad_one, taps_one, 1)
+    begin(over_cores, 1)
+    sum_line(0)
+    sum_cores(1)
     arrive(3, grad_one, taps_back)
-    input_grad[...] = sparse(convolve(taps_back, back[...]).astype(BF16))
+    finish(spread_line, 0)
+    begin(spread_chips, 0)
+    sum_chips(1)
+    result = convolve(taps_back, back[...]).astype(BF16)
+    finish(spread_chips, 0)
+    begin(spread_cores, 0)
+    sum_line(1)
+    input_grad[...] = sparse(result)
+    finish(spread_line, 1)
+    begin(spread_chips, 1)
+    finish(spread_cores, 0)
+    sum_two[...] = total[0]
+    finish(spread_chips, 1)
+    begin(spread_cores, 1)
+    finish(spread_cores, 1)
+    sum_one[...] = total[1]
 
 
 def tap_major(weights):
@@ -274,8 +410,10 @@
     return padded.reshape(LANES, DEPTH)
 
 
-def channel_major(gradient):
-    return gradient.reshape(C, TAPS, LANES)[:, :, :C].transpose(0, 2, 1).reshape(C, C * TAPS)
+def channel_major(total):
+    tiles = total[: TILES * C].reshape(TILES, C, LANES).transpose(1, 0, 2).reshape(C, TILES * LANES)
+    kernel_grad = tiles[:, : C * TAPS].reshape(C, TAPS, C).transpose(0, 2, 1).reshape(C, C * TAPS)
+    return kernel_grad.astype(F32), tiles[:, C * TAPS].astype(F32)
 
 
 def on_device(
@@ -303,13 +441,11 @@
         out_shape=(
             jax.ShapeDtypeStruct((C, ROWS), BF16),
             jax.ShapeDtypeStruct((C, ROWS), BF16),
-            jax.ShapeDtypeStruct((C, DEPTH), F32),
-            jax.ShapeDtypeStruct((C, DEPTH), F32),
-            jax.ShapeDtypeStruct((1, LANES), F32),
-            jax.ShapeDtypeStruct((1, LANES), F32),
+            jax.ShapeDtypeStruct((SUM_ROWS, LANES), BF16),
+            jax.ShapeDtypeStruct((SUM_ROWS, LANES), BF16),
         ),
         in_specs=[vmem] * 8,
-        out_specs=[vmem] * 6,
+        out_specs=[vmem] * 4,
         scratch_shapes=[
             pltpu.VMEM((CELLS, ROWS), BF16),
             pltpu.VMEM((LEVELS * WIDE, LANES), BF16),
@@ -326,8 +462,21 @@
             pltpu.VMEM((4, 128, LANES), BF16),
             pltpu.VMEM((4, sides, 128, LANES), BF16),
             pltpu.VMEM((4, 128, LANES), BF16),
+            pltpu.VMEM((C, TILES * LANES), F32),
+            pltpu.VMEM((2, SUM_ROWS, LANES), F32),
+            pltpu.VMEM((2, SUM_ROWS, LANES), BF16),
+            pltpu.VMEM((2, SUM_ROWS // 2, LANES), BF16),
+            pltpu.VMEM((2, SUM_ROWS // 2, LANES), F32),
+            pltpu.VMEM((2, SUM_ROWS // 2, LANES), BF16),
+            pltpu.VMEM((2, SUM_ROWS // 4, LANES), BF16),
+            pltpu.VMEM((2, SUM_ROWS // 4, LANES), F32),
+            pltpu.VMEM((2, SUM_ROWS // 4, LANES), BF16),
+            pltpu.VMEM((2, parties - 1, SUM_ROWS // 4 // parties, LANES), BF16),
+            pltpu.VMEM((2, SUM_ROWS, LANES), BF16),
             pltpu.SemaphoreType.DMA((4, sides + 1)),
             pltpu.SemaphoreType.DMA((4, sides + 1)),
+            pltpu.SemaphoreType.DMA((2, 2 * parties + 2)),
+            pltpu.SemaphoreType.DMA((2, 2 * parties + 2)),
         ],
         compiler_params=pltpu.CompilerParams(
             collective_id=0, has_side_effects=True, vmem_limit_bytes=48 * 1024 * 1024
@@ -342,16 +491,15 @@
         bias[0],
         bias[1],
     )
-    shards = parties * lax.axis_size("dp") * lax.axis_size("sub")
-    summed = lax.psum(results[2:], ("blocks", "dp", "sub"))
-    scale = 1.0 / shards
+    weight_one_grad, bias_one_grad = channel_major(results[2])
+    weight_two_grad, bias_two_grad = channel_major(results[3])
     return (
         results[0][None],
         results[1][None],
-        channel_major(summed[0]) * scale,
-        channel_major(summed[1]) * scale,
-        summed[2][0, :C] * scale,
-        summed[3][0, :C] * scale,
+        weight_one_grad,
+        weight_two_grad,
+        bias_one_grad,
+        bias_two_grad,
     )
 
 

time: 175 us -> 77.3 us (0.44)
  waiting for transfers between devices: 72 us -> 0 us
  blocking collectives: 30.1 us -> 0 us
  Pallas kernels: 32.2 us -> 54.3 us
  between operations: 14.3 us -> 0.81 us
  local copies, waits for them, and re-layouts: 19.5 us -> 16.6 us
    psum x1 -> x0, waiting for transfers between devices: 72 us -> none  [on_device(): summed = lax.psum(results[2:], ('blocks', 'dp', 'sub'))]
    psum x1 -> x0, blocking collectives: 30.1 us -> none  [on_device(): summed = lax.psum(results[2:], ('blocks', 'dp', 'sub'))]
    pallas_call x1, Pallas kernels: 32.2 us -> 54.3 us  [on_device(): pl.pallas_call(functools.partial(kernel, parties), out_shape=(jax.ShapeDt...]
    reshape x2 -> x0, local copies, waits for them, and re-layouts: 3.99 us -> none  [channel_major(): gradient.reshape(C, TAPS, LANES)[:, :, :C].transpose(0, 2, 1)]
    mul x4 -> x0, local copies, waits for them, and re-layouts: 3.43 us -> none  [the longest x2 1.72 us: on_device(): channel_major(summed[1]) * scale]
    mul x4 -> x0, other arithmetic: 2.75 us -> none  [the longest x1 1.57 us: on_device(): channel_major(summed[0]) * scale]
    convert_element_type x0 -> x4, local copies, waits for them, and re-layouts: none -> 1.77 us  [channel_major(): return (kernel_grad.astype(F32), tiles[:, C * TAPS].astype(F32))]
    unnamed x22 -> x14, local copies, waits for them, and re-layouts: 7.44 us -> 6.3 us
  transfers between devices with their start and end apart: 1 -> 0, of which waited for: 1 -> 0; matrix products, arithmetic and copies ran while one was open for 1% -> 0% of each run, Pallas kernels for 0% -> 0%
where the time goes in v2:
time: 77.3 us; the launch traced here: 77 us
  Pallas kernels  54.3 us (70%)
  local copies, waits for them, and re-layouts  16.6 us (21%)
  other arithmetic  5.26 us (7%)
  between operations  0.81 us (1%)
    pallas_call x1, Pallas kernels, on_device(): pl.pallas_call(functools.partial(kernel, parties), out_shape=(jax.ShapeDt...  54.3 us
    unnamed x14, local copies, waits for them, and re-layouts  6.3 us
    reshape x2, local copies, waits for them, and re-layouts, tap_major(): return padded.reshape(LANES, DEPTH)  2.75 us
    ge x1, other arithmetic, on_device(): flags = jnp.stack([near[0, 1], near[2, 0], near[0, 3], near[1, 2]]) >= 0  2.66 us
    convert_element_type x4, local copies, waits for them, and re-layouts, channel_major(): return (kernel_grad.astype(F32), tiles[:, C * TAPS].astype(F32))  1.77 us

profile of v2, /device:TPU:0, one launch (start us, length us, event | category | flops | bytes accessed | tf_op | source)
XLA Modules:
  0.0 77.0 jit_solution(8887103523032947904)
XLA Ops:
  0.6 0.7 pad_bitcast_fusion
  1.3 0.7 add_bitcast_fusion
  2.0 1.4 %fusion.5 = (s32[1,1]{1,0:T(1,128)}, s32[1,1]{1,0:T(1,128)}, s32[1,1]{1,0:T(1,128)}, s32[1,1]{1,0:T(1,128)}) fusion(s32[4,8]{1,0:T(4,128)} %bitcast.75), kind=kLoop, calls=%fused_computation.16 | loop fusion | bytes 32 | tf_op jit(solution)/shard_map/slice | solution.py:435
  3.4 2.7 %add_compare_fusion = pred[4]{0:T(512)(128)(4,1)S(1)} fusion(s32[1]{0:T(128)} %bitcast.8, s32[1]{0:T(128)} %bitcast.7, s32[1]{0:T(128)} %bitcast.6, s32[1]{0:T(128)} %bitcast.5), kind=kLoop, calls=%fused_computation.13 | loop fusion | flops 16 | bytes 20 | tf_op jit(solution)/shard_map/ge | solution.py:435
  6.1 0.1 broadcast_in_dim.23.flags
  6.2 0.9 %fusion.2 = s32[4,64,2]{2,1,0:T(8,128)S(1)} fusion(s32[4,64]{1,0:T(4,128)} %constant.38, s32[4,64]{1,0:T(4,128)S(1)} %add_bitcast_fusion, s32[4,64]{1,0:T(4,128)} %bitcast.74), kind=kLoop, calls=%fused_computation.6 | loop fusion | flops 2560 | bytes 5120 | tf_op jit(solution)/shard_map/jit(_where)/select_n | solution.py:428
  7.0 0.1 select_n.15.target
  7.2 1.4 %copy.23 = bf16[96,2592]{0,1:T(8,128)(2,1)S(1)} copy(bf16[96,2592]{1,0:T(8,128)(2,1)} %param.13) | data formatting | bytes 995328 | tf_op args[2]
  8.5 0.2 reshape.131
  8.7 0.3 copy.35
  9.0 0.0 copy-start.2
  9.0 0.2 pad.23.clone
  9.3 1.0 %copy.27.weight_one = bf16[128,3456]{1,0:T(8,128)(2,1)S(1)} copy(bf16[128,3456]{0,1:T(8,128)(2,1)S(1)} %bitcast.63) | data formatting | bytes 1769472 | tf_op jit(solution)/shard_map/reshape | solution.py:410
  10.3 0.3 copy.25
  10.6 0.2 reshape.133
  10.8 0.3 copy.36
  11.1 1.1 %pad.24.clone = bf16[128,27,128]{0,2,1:T(8,128)(2,1)} pad(bf16[96,27,96]{0,2,1:T(8,128)(2,1)S(1)} %copy.36, bf16[]{:T(256)} %constant.18.clone.1), padding=0_32x0_0x0_32 | pad | bytes 1382402 | tf_op jit(solution)/shard_map/jit(_pad)/pad | solution.py:409
  12.2 1.7 %copy.28.weight_two = bf16[128,3456]{1,0:T(8,128)(2,1)S(1)} copy(bf16[128,3456]{0,1:T(8,128)(2,1)} %bitcast.62) | data formatting | bytes 1769472 | tf_op jit(solution)/shard_map/reshape | solution.py:410
  14.0 54.3 %shard_map.154 = (bf16[96,512]{1,0:T(8,128)(2,1)S(1)}, bf16[96,512]{1,0:T(8,128)(2,1)S(1)}, bf16[2048,128]{1,0:T(8,128)(2,1)S(1)}, bf16[2048,128]{1,0:T(8,128)(2,1)S(1)}) custom-call(bf16[96,512]{1,0:T(8,128)(2,1)S(1)} %bitcast.56, bf16[96,512]{1,0:T(8,128)(2,1)S(1)} %bitcast.57, s32[1,512]{1,0:T(1,128)S(1)} %select_n.15.target, ...), custom_call_target="tpu_custom_call" | custom-call | tf_op jit(solution)/shard_map/pallas_call | solution.py:439
  68.4 0.4 copy.29
  68.7 0.5 fusion.4
  69.3 0.9 %slice.40 = bf16[96,2592]{0,1:T(8,128)(2,1)} slice(bf16[96,2688]{0,1:T(8,128)(2,1)S(1)} %bitcast.67), slice={[0:96], [0:2592]} | slice | bytes 995328 | tf_op jit(solution)/shard_map/slice | solution.py:415
  70.2 0.4 copy.31
  70.5 0.5 fusion.3
  71.1 0.2 copy.39
  71.4 0.1 reshape.140
  71.5 1.4 %copy.34 = f32[96,2592]{1,0:T(8,128)} copy(f32[96,2592]{0,1:T(8,128)S(1)} %reshape.140) | data formatting | bytes 1990656
  72.9 1.3 %copy.40 = f32[96,27,96]{0,1,2:T(8,128)S(1)} copy(bf16[96,27,96]{0,2,1:T(8,128)(2,1)} %bitcast.70) | data formatting | bytes 1492992 | tf_op jit(solution)/shard_map/convert_element_type | solution.py:416
  74.2 0.1 reshape.139
  74.3 1.4 %copy.33 = f32[96,2592]{1,0:T(8,128)} copy(f32[96,2592]{0,1:T(8,128)S(1)} %reshape.139) | data formatting | bytes 1990656
  75.7 0.6 copy.43
  76.3 0.6 copy.44
  (9 shorter events, 0.1 us)
Async XLA Ops:
  9.0 1.3 %copy-start.2 = (bf16[96,2592]{1,0:T(8,128)(2,1)S(1)}, bf16[96,2592]{1,0:T(8,128)(2,1)}, u32[]{:S(2)}) copy-start(bf16[96,2592]{1,0:T(8,128)(2,1)} %param.14) | copy-start | bytes 1492996
  11.1 2.9 %copy-start = (bf16[1,96,512]{2,1,0:T(8,128)(2,1)S(1)}, bf16[1,96,512]{2,1,0:T(8,128)(2,1)}, u32[]{:S(2)}) copy-start(bf16[1,96,512]{2,1,0:T(8,128)(2,1)} %param.11) | copy-start | bytes 294916
  11.1 2.9 %copy-start.1 = (bf16[1,96,512]{2,1,0:T(8,128)(2,1)S(1)}, bf16[1,96,512]{2,1,0:T(8,128)(2,1)}, u32[]{:S(2)}) copy-start(bf16[1,96,512]{2,1,0:T(8,128)(2,1)} %param.12) | copy-start | bytes 294916

commit v3 on v2

--- a/solution.py
+++ b/solution.py
@@ -2,7 +2,6 @@
 
 import jax
 import jax.numpy as jnp
-import numpy as np
 from jax import lax
 from jax.experimental import pallas as pl
 from jax.experimental.pallas import tpu as pltpu
@@ -58,21 +57,28 @@
     parties,
     features,
     grad_out,
-    target,
-    flags,
     weight_one,
     weight_two,
     bias_one,
     bias_two,
+    heights,
+    counts,
+    neighbours,
     out_features,
     input_grad,
-    sum_one,
-    sum_two,
+    weight_one_grad,
+    weight_two_grad,
+    bias_one_grad,
+    bias_two_grad,
     place,
     spread_left,
     spread_right,
     pick,
-    turned,
+    square,
+    strided,
+    taken_one,
+    taken_two,
+    bias_kept,
     back,
     taps_one,
     taps_two,
@@ -83,7 +89,6 @@
     send_across,
     got_side,
     got_across,
-    packed,
     part,
     part_sent,
     got_core,
@@ -112,7 +117,19 @@
     for partner in partners:
         pl.semaphore_signal(barrier, inc=1, device_id=partner, device_id_type=MESH)
 
-    place[...] = one_hot(iota((CELLS, ROWS), 0) == target[...])
+    lane = iota((SIDE * SIDE, LANES), 1)
+    double = one_hot(lane // KMAX == iota((SIDE * SIDE, LANES), 0))
+    low = dot(heights[0].astype(F32).astype(BF16), double).astype(jnp.int32)
+    held = dot(counts[0].astype(F32).astype(BF16), double).astype(jnp.int32)
+    lane = iota((1, LANES), 1)
+    column = lane // KMAX
+    layer = lane % KMAX
+    cell_at = iota((CELLS, LANES), 0)
+    for slot in range(4):
+        cell = (SIDE * (slot // 2) + column // SIDE) * EDGE + SIDE * (slot % 2) + column % SIDE
+        target = (low[slot : slot + 1] - LOW + layer) * PLANE + cell
+        target = jnp.where(layer < held[slot : slot + 1], target, -1)
+        place[:, slot * LANES : (slot + 1) * LANES] = one_hot(cell_at == target)
     mask_kept[...] = dot(place[...], jnp.ones((ROWS, LANES), BF16))
 
     row = iota((LEVELS * WIDE, LANES), 0)
@@ -141,7 +158,7 @@
         part_sent[layer, TILES * C :] = jnp.zeros((spare, LANES), BF16)
 
     def dense(rows_ref):
-        padded = jnp.concatenate([rows_ref[...], jnp.zeros((LANES - C, ROWS), BF16)], axis=0)
+        padded = jnp.concatenate([rows_ref[0], jnp.zeros((LANES - C, ROWS), BF16)], axis=0)
         return dot(place[...], padded, ((1,), (1,))).astype(BF16)
 
     def sparse(cells):
@@ -182,10 +199,10 @@
         for copy in copies(turn):
             copy.start()
 
-    up = flags[0:1] > 0
-    down = flags[1:2] > 0
-    left = flags[2:3] > 0
-    right = flags[3:4] > 0
+    def there(slot, direction):
+        return jnp.broadcast_to(neighbours[0, slot : slot + 1, direction : direction + 1], (1, LANES)) >= 0
+
+    up, down, left, right = there(0, 1), there(2, 0), there(0, 3), there(1, 2)
 
     def arrive(turn, cells, taps):
         for copy in copies(turn):
@@ -237,20 +254,20 @@
         return jnp.concatenate(results, axis=0)
 
     def weight_grad(gradient, taps, layer):
-        flipped = jnp.transpose(gradient)[:C]
+        flipped = jnp.transpose(gradient)
         for dz in range(3):
             for dx in range(3):
                 field = jnp.concatenate(
                     [taps[z + dz, dx * EDGE : dx * EDGE + PLANE] for z in range(LEVELS)], axis=0
                 )
-                product = dot(flipped, field)
+                product = jnp.transpose(dot(flipped, field))
                 for dy in range(3):
-                    first = ((3 * dz + dx) * 3 + dy) * C
-                    packed[:, first : first + C] = product[:, dy * LANES : dy * LANES + C]
-        bias = dot(flipped, jnp.ones((CELLS, LANES), BF16))
-        packed[:, TAPS * C : (TAPS + 1) * C] = bias[:, :C]
+                    tap = (3 * dz + dx) * 3 + dy
+                    strided[pl.ds(tap, C, stride=TAPS), :] = product[dy * LANES : dy * LANES + C]
+        bias = jnp.sum(gradient.astype(F32), axis=0, keepdims=True)
+        strided[TAPS * C :] = jnp.broadcast_to(bias, (C, LANES))
         for tile in range(TILES):
-            piece = packed[:, tile * LANES : (tile + 1) * LANES]
+            piece = jnp.transpose(strided[tile * LANES : (tile + 1) * LANES])[:C]
             part[layer, tile * C : (tile + 1) * C] = piece
             part_sent[layer, tile * C : (tile + 1) * C] = piece.astype(BF16)
 
@@ -343,34 +360,56 @@
         total[layer, pl.ds(pl.multiple_of(mine + me * share, 16), share)] = value.astype(BF16)
         begin(spread_line, layer)
 
-    def turn_back(weights):
+    def take_taps(weights, taken):
+        square[:C, : TAPS * C] = weights[...].astype(F32)
+        for tile in range(TILES):
+            part_of = slice(tile * LANES, (tile + 1) * LANES)
+            strided[part_of] = jnp.transpose(square[:, part_of])
+        for tap in range(TAPS):
+            rows = strided[pl.ds(tap, C, stride=TAPS), :]
+            taken[tap * LANES : tap * LANES + C] = rows.astype(BF16)
+            taken[tap * LANES + C : (tap + 1) * LANES] = jnp.zeros((LANES - C, LANES), BF16)
+
+    def turn_back(taken):
         for tap in range(TAPS):
             other = TAPS - 1 - tap
-            back[tap * LANES : (tap + 1) * LANES] = weights[
-                :, other * LANES : (other + 1) * LANES
-            ]
-
+            tile = taken[other * LANES : (other + 1) * LANES]
+            back[tap * LANES : (tap + 1) * LANES] = jnp.transpose(tile)
+
+    def hand_out(layer, weights_out, bias_out):
+        for tile in range(TILES - 1):
+            piece = total[layer, tile * C : (tile + 1) * C]
+            weights_out[:, tile * LANES : (tile + 1) * LANES] = piece.astype(F32)
+        last = total[layer, (TILES - 1) * C :].astype(F32)
+        rest = TAPS * C - (TILES - 1) * LANES
+        weights_out[:, (TILES - 1) * LANES :] = last[:C, :rest]
+        bias_out[...] = jnp.transpose(last)[rest : rest + 1, :C]
+
+    square[...] = jnp.zeros((LANES, TILES * LANES), F32)
+    bias_kept[...] = jnp.zeros((2, 1, LANES), F32)
+    bias_kept[0, :, :C] = bias_one[...]
+    bias_kept[1, :, :C] = bias_two[...]
     live = mask_kept[...] > 0
     cells = dense(features)
     pl.semaphore_wait(barrier, len(partners))
     send(0, cells)
-    turned[...] = jnp.transpose(weight_one[...])
+    take_taps(weight_one, taken_one)
     arrive(0, cells, taps_one)
 
-    pre_one = convolve(taps_one, turned[...]) + bias_one[...]
+    pre_one = convolve(taps_one, taken_one[...]) + bias_kept[0]
     pre_kept[...] = pre_one
     hidden = jnp.where(live, pre_one * jax.nn.sigmoid(pre_one), 0.0).astype(BF16)
     send(1, hidden)
-    turned[...] = jnp.transpose(weight_two[...])
+    take_taps(weight_two, taken_two)
     upstream = dense(grad_out)
-    turn_back(weight_two)
+    turn_back(taken_two)
     arrive(1, hidden, taps_two)
 
-    pre_two = convolve(taps_two, turned[...]) + bias_two[...]
+    pre_two = convolve(taps_two, taken_two[...]) + bias_kept[1]
     grad_two = jnp.where(live, upstream.astype(F32) * slope_of(pre_two), 0.0).astype(BF16)
     send(2, grad_two)
     activated = jnp.where(live, pre_two * jax.nn.sigmoid(pre_two), 0.0).astype(BF16)
-    out_features[...] = sparse(activated)
+    out_features[0] = sparse(activated)
     weight_grad(grad_two, taps_two, 0)
     begin(over_cores, 0)
     arrive(2, grad_two, taps_back)
@@ -380,7 +419,7 @@
     grad_one = jnp.where(live, hidden_sum * slope_of(pre_kept[...]), 0.0).astype(BF16)
     send(3, grad_one)
     sum_chips(0)
-    turn_back(weight_one)
+    turn_back(taken_one)
     weight_grad(grad_one, taps_one, 1)
     begin(over_cores, 1)
     sum_line(0)
@@ -393,27 +432,15 @@
     finish(spread_chips, 0)
     begin(spread_cores, 0)
     sum_line(1)
-    input_grad[...] = sparse(result)
+    input_grad[0] = sparse(result)
     finish(spread_line, 1)
     begin(spread_chips, 1)
     finish(spread_cores, 0)
-    sum_two[...] = total[0]
+    hand_out(0, weight_two_grad, bias_two_grad)
     finish(spread_chips, 1)
     begin(spread_cores, 1)
     finish(spread_cores, 1)
-    sum_one[...] = total[1]
-
-
-def tap_major(weights):
-    kernel_taps = weights.reshape(C, C, TAPS).transpose(0, 2, 1)
-    padded = jnp.pad(kernel_taps, ((0, LANES - C), (0, 0), (0, LANES - C)))
-    return padded.reshape(LANES, DEPTH)
-
-
-def channel_major(total):
-    tiles = total[: TILES * C].reshape(TILES, C, LANES).transpose(1, 0, 2).reshape(C, TILES * LANES)
-    kernel_grad = tiles[:, : C * TAPS].reshape(C, TAPS, C).transpose(0, 2, 1).reshape(C, C * TAPS)
-    return kernel_grad.astype(F32), tiles[:, C * TAPS].astype(F32)
+    hand_out(1, weight_one_grad, bias_one_grad)
 
 
 def on_device(
@@ -421,37 +448,29 @@
 ):
     parties = lax.axis_size("blocks")
     sides = len(side_offsets(parties))
-    block = np.arange(4)[:, None]
-    column = np.arange(SIDE * SIDE)[None, :]
-    cell = (SIDE * (block // 2) + column // SIDE) * EDGE + SIDE * (block % 2) + column % SIDE
-    layer = np.arange(KMAX)[None, None, :]
-    target = jnp.where(
-        layer < counts[0][:, :, None],
-        (heights[0][:, :, None] - LOW + layer) * PLANE + cell[:, :, None],
-        -1,
-    )
-    target = target.astype(jnp.int32).reshape(1, ROWS)
-    near = neighbours[0]
-    flags = jnp.stack([near[0, 1], near[2, 0], near[0, 3], near[1, 2]]) >= 0
-    flags = jnp.broadcast_to(jnp.pad(flags.astype(jnp.int32), (0, 4))[:, None], (8, LANES))
-    bias = [jnp.pad(value, (0, LANES - C))[None] for value in (bias_one, bias_two)]
     vmem = pl.BlockSpec(memory_space=pltpu.VMEM)
     results = pl.pallas_call(
         functools.partial(kernel, parties),
         out_shape=(
-            jax.ShapeDtypeStruct((C, ROWS), BF16),
-            jax.ShapeDtypeStruct((C, ROWS), BF16),
-            jax.ShapeDtypeStruct((SUM_ROWS, LANES), BF16),
-            jax.ShapeDtypeStruct((SUM_ROWS, LANES), BF16),
+            jax.ShapeDtypeStruct((1, C, ROWS), BF16),
+            jax.ShapeDtypeStruct((1, C, ROWS), BF16),
+            jax.ShapeDtypeStruct((C, TAPS * C), F32),
+            jax.ShapeDtypeStruct((C, TAPS * C), F32),
+            jax.ShapeDtypeStruct((1, C), F32),
+            jax.ShapeDtypeStruct((1, C), F32),
         ),
-        in_specs=[vmem] * 8,
-        out_specs=[vmem] * 4,
+        in_specs=[vmem] * 9,
+        out_specs=[vmem] * 6,
         scratch_shapes=[
             pltpu.VMEM((CELLS, ROWS), BF16),
             pltpu.VMEM((LEVELS * WIDE, LANES), BF16),
             pltpu.VMEM((LEVELS * WIDE, LANES), BF16),
             pltpu.VMEM((128, CELLS), BF16),
+            pltpu.VMEM((LANES, TILES * LANES), F32),
+            pltpu.VMEM((TILES * LANES, LANES), F32),
             pltpu.VMEM((DEPTH, LANES), BF16),
+            pltpu.VMEM((DEPTH, LANES), BF16),
+            pltpu.VMEM((2, 1, LANES), F32),
             pltpu.VMEM((DEPTH, LANES), BF16),
             pltpu.VMEM((LEVELS + 2, WIDE, 3 * LANES), BF16),
             pltpu.VMEM((LEVELS + 2, WIDE, 3 * LANES), BF16),
@@ -462,7 +481,6 @@
             pltpu.VMEM((4, 128, LANES), BF16),
             pltpu.VMEM((4, sides, 128, LANES), BF16),
             pltpu.VMEM((4, 128, LANES), BF16),
-            pltpu.VMEM((C, TILES * LANES), F32),
             pltpu.VMEM((2, SUM_ROWS, LANES), F32),
             pltpu.VMEM((2, SUM_ROWS, LANES), BF16),
             pltpu.VMEM((2, SUM_ROWS // 2, LANES), BF16),
@@ -482,25 +500,17 @@
             collective_id=0, has_side_effects=True, vmem_limit_bytes=48 * 1024 * 1024
         ),
     )(
-        features[0],
-        grad_out[0],
-        target,
-        flags,
-        tap_major(weight_one),
-        tap_major(weight_two),
-        bias[0],
-        bias[1],
+        features,
+        grad_out,
+        weight_one,
+        weight_two,
+        bias_one[None],
+        bias_two[None],
+        heights,
+        counts,
+        neighbours,
     )
-    weight_one_grad, bias_one_grad = channel_major(results[2])
-    weight_two_grad, bias_two_grad = channel_major(results[3])
-    return (
-        results[0][None],
-        results[1][None],
-        weight_one_grad,
-        weight_two_grad,
-        bias_one_grad,
-        bias_two_grad,
-    )
+    return (*results[:4], results[4][0], results[5][0])
 
 
 def solution(mesh):

time: 77.3 us -> 64.5 us (0.83)
  local copies, waits for them, and re-layouts: 16.6 us -> 10.1 us
  other arithmetic: 5.26 us -> 0 us
  Pallas kernels: 54.3 us -> 53.3 us
    unnamed x14 -> x24, local copies, waits for them, and re-layouts: 6.3 us -> 10.1 us
    reshape x4 -> x0, local copies, waits for them, and re-layouts: 3.13 us -> none  [the longest x2 2.75 us: tap_major(): return padded.reshape(LANES, DEPTH)]
    ge x1 -> x0, other arithmetic: 2.66 us -> none  [on_device(): flags = jnp.stack([near[0, 1], near[2, 0], near[0, 3], near[1, 2]]) >= 0]
    slice x5 -> x0, local copies, waits for them, and re-layouts: 2.42 us -> none  [the longest x1 1.42 us: on_device(): flags = jnp.stack([near[0, 1], near[2, 0], near[0, 3], near[1, 2]]) >= 0]
    convert_element_type x4 -> x0, local copies, waits for them, and re-layouts: 1.77 us -> none  [channel_major(): return (kernel_grad.astype(F32), tiles[:, C * TAPS].astype(F32))]
    pad x2 -> x0, local copies, waits for them, and re-layouts: 1.37 us -> none  [tap_major(): padded = jnp.pad(kernel_taps, ((0, LANES - C), (0, 0), (0, LANES - C)))]
    convert_element_type x2 -> x0, other arithmetic: 1.04 us -> none  [channel_major(): return (kernel_grad.astype(F32), tiles[:, C * TAPS].astype(F32))]
    pallas_call x1, Pallas kernels: 54.3 us -> 53.3 us  [on_device(): pl.pallas_call(functools.partial(kernel, parties), out_shape=(jax.ShapeDt...]
where the time goes in v3:
time: 64.5 us; the launch traced here: 64.1 us
  Pallas kernels  53.3 us (83%)
  local copies, waits for them, and re-layouts  10.1 us (16%)
  between operations  0.68 us (1%)
    pallas_call x1, Pallas kernels, on_device(): pl.pallas_call(functools.partial(kernel, parties), out_shape=(jax.ShapeDt...  53.3 us
    unnamed x24, local copies, waits for them, and re-layouts  10.1 us

profile of v3, /device:TPU:0, one launch (start us, length us, event | category | flops | bytes accessed | tf_op | source)
XLA Modules:
  0.0 64.1 jit_solution(18084699583224120412)
XLA Ops:
  0.6 0.0 copy-start.4
  0.6 0.0 copy-start.7
  0.7 0.0 copy-start.8
  0.7 0.7 %copy-done.4 = s32[1,4,64]{2,1,0:T(4,128)S(1)} copy-done((s32[1,4,64]{2,1,0:T(4,128)S(1)}, s32[1,4,64]{2,1,0:T(4,128)}, u32[]{:S(2)}) %copy-start.4) | copy-done | bytes 1048
  1.3 0.0 copy-done.7
  1.3 0.0 copy-done.8
  1.3 0.0 copy-start
  1.3 1.0 %copy-done = bf16[96,2592]{1,0:T(8,128)(2,1)S(1)} copy-done((bf16[96,2592]{1,0:T(8,128)(2,1)S(1)}, bf16[96,2592]{1,0:T(8,128)(2,1)}, u32[]{:S(2)}) %copy-start) | copy-done | bytes 497688
  2.4 0.0 copy-start.1
  2.4 1.0 %copy-done.1 = bf16[96,2592]{1,0:T(8,128)(2,1)S(1)} copy-done((bf16[96,2592]{1,0:T(8,128)(2,1)S(1)}, bf16[96,2592]{1,0:T(8,128)(2,1)}, u32[]{:S(2)}) %copy-start.1) | copy-done | bytes 497688
  3.4 0.0 copy-start.2
  3.4 0.9 %copy-done.2 = bf16[1,96,512]{2,1,0:T(8,128)(2,1)S(1)} copy-done((bf16[1,96,512]{2,1,0:T(8,128)(2,1)S(1)}, bf16[1,96,512]{2,1,0:T(8,128)(2,1)}, u32[]{:S(2)}) %copy-start.2) | copy-done | bytes 98328
  4.3 0.0 copy-start.3
  4.3 0.9 %copy-done.3 = bf16[1,96,512]{2,1,0:T(8,128)(2,1)S(1)} copy-done((bf16[1,96,512]{2,1,0:T(8,128)(2,1)S(1)}, bf16[1,96,512]{2,1,0:T(8,128)(2,1)}, u32[]{:S(2)}) %copy-start.3) | copy-done | bytes 98328
  5.2 0.0 copy-start.5
  5.2 0.7 %copy-done.5 = s32[1,4,64]{2,1,0:T(4,128)S(1)} copy-done((s32[1,4,64]{2,1,0:T(4,128)S(1)}, s32[1,4,64]{2,1,0:T(4,128)}, u32[]{:S(2)}) %copy-start.5) | copy-done | bytes 1048
  5.9 0.0 copy-start.6
  5.9 0.7 %copy-done.6 = s32[1,4,8]{2,1,0:T(4,128)S(1)} copy-done((s32[1,4,8]{2,1,0:T(4,128)S(1)}, s32[1,4,8]{2,1,0:T(4,128)}, u32[]{:S(2)}) %copy-start.6) | copy-done | bytes 152
  6.6 53.3 %shard_map.136 = (bf16[1,96,512]{2,1,0:T(8,128)(2,1)S(1)}, bf16[1,96,512]{2,1,0:T(8,128)(2,1)S(1)}, f32[96,2592]{1,0:T(8,128)S(1)}, f32[96,2592]{1,0:T(8,128)S(1...) custom-call(bf16[1,96,512]{2,1,0:T(8,128)(2,1)S(1)} %copy-done.2, bf16[1,96,512]{2,1,0:T(8,128)(2,1)S(1)} %copy-done.3, ...), custom_call_target="tpu_custom_call" | custom-call | tf_op jit(solution)/shard_map/pallas_call | solution.py:452
  59.9 0.6 %copy.21 = bf16[1,96,512]{2,1,0:T(8,128)(2,1)} copy(bf16[1,96,512]{2,1,0:T(8,128)(2,1)S(1)} %get-tuple-element.24) | data formatting | bytes 196608
  60.5 0.6 copy.22
  61.2 1.0 %copy.23 = f32[96,2592]{1,0:T(8,128)} copy(f32[96,2592]{1,0:T(8,128)S(1)} %get-tuple-element.26) | data formatting | bytes 1990656
  62.1 1.0 %copy.24 = f32[96,2592]{1,0:T(8,128)} copy(f32[96,2592]{1,0:T(8,128)S(1)} %get-tuple-element.27) | data formatting | bytes 1990656
  63.1 0.5 copy.25
  63.6 0.5 copy.26
Async XLA Ops:
  0.6 0.7 %copy-start.4 = (s32[1,4,64]{2,1,0:T(4,128)S(1)}, s32[1,4,64]{2,1,0:T(4,128)}, u32[]{:S(2)}) copy-start(s32[1,4,64]{2,1,0:T(4,128)} %heights.1) | copy-start | bytes 3076
  0.6 0.7 %copy-start.7 = (f32[96]{0:T(128)S(1)}, f32[96]{0:T(128)}, u32[]{:S(2)}) copy-start(f32[96]{0:T(128)} %param.13) | copy-start | bytes 1156
  0.7 0.7 %copy-start.8 = (f32[96]{0:T(128)S(1)}, f32[96]{0:T(128)}, u32[]{:S(2)}) copy-start(f32[96]{0:T(128)} %param.14) | copy-start | bytes 1156
  1.3 1.0 %copy-start = (bf16[96,2592]{1,0:T(8,128)(2,1)S(1)}, bf16[96,2592]{1,0:T(8,128)(2,1)}, u32[]{:S(2)}) copy-start(bf16[96,2592]{1,0:T(8,128)(2,1)} %weight_one.1) | copy-start | bytes 1492996
  2.4 1.0 %copy-start.1 = (bf16[96,2592]{1,0:T(8,128)(2,1)S(1)}, bf16[96,2592]{1,0:T(8,128)(2,1)}, u32[]{:S(2)}) copy-start(bf16[96,2592]{1,0:T(8,128)(2,1)} %weight_two.1) | copy-start | bytes 1492996
  3.4 0.9 %copy-start.2 = (bf16[1,96,512]{2,1,0:T(8,128)(2,1)S(1)}, bf16[1,96,512]{2,1,0:T(8,128)(2,1)}, u32[]{:S(2)}) copy-start(bf16[1,96,512]{2,1,0:T(8,128)(2,1)} %features.1) | copy-start | bytes 294916
  4.3 0.9 %copy-start.3 = (bf16[1,96,512]{2,1,0:T(8,128)(2,1)S(1)}, bf16[1,96,512]{2,1,0:T(8,128)(2,1)}, u32[]{:S(2)}) copy-start(bf16[1,96,512]{2,1,0:T(8,128)(2,1)} %grad_out.1) | copy-start | bytes 294916
  5.2 0.7 %copy-start.5 = (s32[1,4,64]{2,1,0:T(4,128)S(1)}, s32[1,4,64]{2,1,0:T(4,128)}, u32[]{:S(2)}) copy-start(s32[1,4,64]{2,1,0:T(4,128)} %counts.1) | copy-start | bytes 3076
  5.9 0.7 %copy-start.6 = (s32[1,4,8]{2,1,0:T(4,128)S(1)}, s32[1,4,8]{2,1,0:T(4,128)}, u32[]{:S(2)}) copy-start(s32[1,4,8]{2,1,0:T(4,128)} %neighbours.1) | copy-start | bytes 388

commit v4 on v3

--- a/solution.py
+++ b/solution.py
@@ -36,6 +36,10 @@
     return found
 
 
+def stream_count(parties):
+    return 2 if SUM_ROWS // 8 // parties % 16 == 0 else 1
+
+
 def dot(left, right, dims=((1,), (0,))):
     return lax.dot_general(left, right, (dims, ((), ())), preferred_element_type=F32)
 
@@ -55,61 +59,85 @@
 
 def kernel(
     parties,
-    features,
-    grad_out,
-    weight_one,
-    weight_two,
-    bias_one,
-    bias_two,
-    heights,
-    counts,
-    neighbours,
-    out_features,
-    input_grad,
-    weight_one_grad,
-    weight_two_grad,
-    bias_one_grad,
-    bias_two_grad,
-    place,
-    spread_left,
-    spread_right,
-    pick,
-    square,
-    strided,
-    taken_one,
-    taken_two,
-    bias_kept,
-    back,
-    taps_one,
-    taps_two,
-    taps_back,
-    pre_kept,
-    mask_kept,
-    send_side,
-    send_across,
-    got_side,
-    got_across,
-    part,
-    part_sent,
-    got_core,
-    core_sum,
-    core_sent,
-    got_chip,
-    chip_sum,
-    chip_sent,
-    got_line,
-    total,
-    send_sem,
-    recv_sem,
-    sum_send,
-    sum_recv,
+    *refs,
 ):
+    given, refs = refs[:9], refs[9:]
+    results, refs = refs[:6], refs[6:]
+    held_in, refs = refs[:9], refs[9:]
+    held_out, refs = refs[:6], refs[6:]
+    (
+        features,
+        grad_out,
+        weight_one,
+        weight_two,
+        bias_one,
+        bias_two,
+        heights,
+        counts,
+        neighbours,
+    ) = held_in
+    (
+        out_features,
+        input_grad,
+        weight_one_grad,
+        weight_two_grad,
+        bias_one_grad,
+        bias_two_grad,
+    ) = held_out
+    (
+        place,
+        spread_left,
+        spread_right,
+        pick,
+        square,
+        strided,
+        taken_one,
+        taken_two,
+        bias_kept,
+        back,
+        taps_one,
+        taps_two,
+        taps_back,
+        pre_kept,
+        mask_kept,
+        send_side,
+        send_across,
+        got_side,
+        got_across,
+        part,
+        part_sent,
+        got_core,
+        core_sum,
+        core_sent,
+        got_chip,
+        chip_sum,
+        chip_sent,
+        got_line,
+        total,
+        send_sem,
+        recv_sem,
+        sum_send,
+        sum_recv,
+        in_sem,
+        out_sem,
+    ) = refs
+
+    def bring(number):
+        return pltpu.make_async_copy(given[number], held_in[number], in_sem.at[number])
+
+    def leave(number):
+        return pltpu.make_async_copy(held_out[number], results[number], out_sem.at[number])
+
+    for number in (6, 7, 8, 0, 2, 4, 5, 3, 1):
+        bring(number).start()
     offsets = side_offsets(parties)
     half = parties // 2
     me = lax.axis_index("blocks")
     chip = lax.axis_index("dp")
     core = lax.axis_index("sub")
-    share = SUM_ROWS // 4 // parties
+    streams = stream_count(parties)
+    span = SUM_ROWS // streams
+    share = span // 4 // parties
     partners = [{"blocks": lax.rem(me + offset, parties)} for offset in range(1, parties)]
     partners += [{"dp": 1 - chip}, {"sub": 1 - core}]
 
@@ -117,6 +145,8 @@
     for partner in partners:
         pl.semaphore_signal(barrier, inc=1, device_id=partner, device_id_type=MESH)
 
+    for number in (6, 7, 8):
+        bring(number).wait()
     lane = iota((SIDE * SIDE, LANES), 1)
     double = one_hot(lane // KMAX == iota((SIDE * SIDE, LANES), 0))
     low = dot(heights[0].astype(F32).astype(BF16), double).astype(jnp.int32)
@@ -169,7 +199,7 @@
         for slot, offset in enumerate(offsets):
             result.append(
                 pltpu.make_async_remote_copy(
-                    src_ref=send_side.at[turn],
+                    src_ref=send_side.at[turn, slot],
                     dst_ref=got_side.at[turn, slot],
                     send_sem=send_sem.at[turn, slot],
                     recv_sem=recv_sem.at[turn, slot],
@@ -190,12 +220,18 @@
         return result
 
     def send(turn, cells):
-        send_side[turn] = dot(pick[...], cells).astype(BF16)
+        both = dot(pick[...], cells)
+        first, last = both[:64], both[64:]
+        to_right = jnp.where(right, last, first).astype(BF16)
+        to_left = jnp.where(left, first, last).astype(BF16)
+        for slot, offset in enumerate(offsets):
+            rightward = offset == 1 or (offset != parties - 1 and offset == half + 1)
+            send_side[turn, slot] = to_right if rightward else to_left
         for z in range(LEVELS):
-            send_across[turn, z * EDGE : (z + 1) * EDGE] = cells[z * PLANE : z * PLANE + EDGE]
-            send_across[turn, 64 + z * EDGE : 64 + (z + 1) * EDGE] = cells[
-                (z + 1) * PLANE - EDGE : (z + 1) * PLANE
-            ]
+            first = cells[z * PLANE : z * PLANE + EDGE].astype(F32)
+            last = cells[(z + 1) * PLANE - EDGE : (z + 1) * PLANE].astype(F32)
+            chosen = jnp.where(up, first, last).astype(BF16)
+            send_across[turn, z * EDGE : (z + 1) * EDGE] = chosen
         for copy in copies(turn):
             copy.start()
 
@@ -210,9 +246,9 @@
         inside = iota((64, LANES), 0) % EDGE
         corner = ((inside == EDGE - 1) & up) | ((inside == 0) & down)
 
-        def columns(main, diagonal, first, there):
-            straight = got_side[turn, offsets.index(main), first : first + 64]
-            slanted = got_side[turn, offsets.index(diagonal), first : first + 64]
+        def columns(main, diagonal, there):
+            straight = got_side[turn, offsets.index(main)]
+            slanted = got_side[turn, offsets.index(diagonal)]
             both = jnp.concatenate(
                 [
                     jnp.where(there, straight.astype(F32), 0.0),
@@ -222,15 +258,14 @@
             )
             return both.astype(BF16)
 
-        from_left = columns(1, (half + 1) % parties, 64, left)
-        from_right = columns(parties - 1, (half - 1) % parties, 0, right)
+        from_left = columns(1, (half + 1) % parties, left)
+        from_right = columns(parties - 1, (half - 1) % parties, right)
         pieces = []
         for z in range(LEVELS):
-            above = got_across[turn, 64 + z * EDGE : 64 + (z + 1) * EDGE].astype(F32)
-            below = got_across[turn, z * EDGE : (z + 1) * EDGE].astype(F32)
-            pieces.append(jnp.where(up, above, 0.0))
+            beside = got_across[turn, z * EDGE : (z + 1) * EDGE].astype(F32)
+            pieces.append(jnp.where(up, beside, 0.0))
             pieces.append(cells[z * PLANE : (z + 1) * PLANE].astype(F32))
-            pieces.append(jnp.where(down, below, 0.0))
+            pieces.append(jnp.where(down, beside, 0.0))
         middle = jnp.concatenate(pieces, axis=0)
         place_along = iota((LEVELS * WIDE, LANES), 0) % EDGE
         before = jnp.where(place_along == 0, 0.0, pltpu.roll(middle, 1, 0))
@@ -271,94 +306,99 @@
             part[layer, tile * C : (tile + 1) * C] = piece
             part_sent[layer, tile * C : (tile + 1) * C] = piece.astype(BF16)
 
-    half_rows, quarter = SUM_ROWS // 2, SUM_ROWS // 4
+    half_rows, quarter = span // 2, span // 4
+
+    def from_row(stream, row, length):
+        first = pl.multiple_of((stream % streams) * span + row, 16)
+        return stream // streams, pl.ds(first, length)
+
     mine = core * half_rows + chip * quarter
 
-    def remote(source, landing, layer, number, partner):
+    def remote(source, landing, stream, number, partner):
         return pltpu.make_async_remote_copy(
             src_ref=source,
             dst_ref=landing,
-            send_sem=sum_send.at[layer, number],
-            recv_sem=sum_recv.at[layer, number],
+            send_sem=sum_send.at[stream, number],
+            recv_sem=sum_recv.at[stream, number],
             device_id=partner,
             device_id_type=MESH,
         )
 
-    def over_cores(layer):
-        other = pl.ds(pl.multiple_of((1 - core) * half_rows, 16), half_rows)
+    def over_cores(stream):
+        other = from_row(stream, (1 - core) * half_rows, half_rows)
         return [
-            remote(part_sent.at[layer, other], got_core.at[layer], layer, 0, {"sub": 1 - core})
+            remote(part_sent.at[other], got_core.at[stream], stream, 0, {"sub": 1 - core})
         ]
 
-    def over_chips(layer):
+    def over_chips(stream):
         other = pl.ds(pl.multiple_of((1 - chip) * quarter, 16), quarter)
         return [
-            remote(core_sent.at[layer, other], got_chip.at[layer], layer, 1, {"dp": 1 - chip})
+            remote(core_sent.at[stream, other], got_chip.at[stream], stream, 1, {"dp": 1 - chip})
         ]
 
-    def over_line(layer):
+    def over_line(stream):
         result = []
         for offset in range(1, parties):
             there = lax.rem(me + offset, parties)
             rows = pl.ds(pl.multiple_of(there * share, 16), share)
             result.append(
                 remote(
-                    chip_sent.at[layer, rows],
-                    got_line.at[layer, offset - 1],
-                    layer,
+                    chip_sent.at[stream, rows],
+                    got_line.at[stream, offset - 1],
+                    stream,
                     1 + offset,
                     {"blocks": there},
                 )
             )
         return result
 
-    def spread_line(layer):
-        rows = total.at[layer, pl.ds(pl.multiple_of(mine + me * share, 16), share)]
+    def spread_line(stream):
+        rows = total.at[from_row(stream, mine + me * share, share)]
         return [
-            remote(rows, rows, layer, parties + offset, {"blocks": lax.rem(me + offset, parties)})
+            remote(rows, rows, stream, parties + offset, {"blocks": lax.rem(me + offset, parties)})
             for offset in range(1, parties)
         ]
 
-    def spread_chips(layer):
-        rows = total.at[layer, pl.ds(pl.multiple_of(mine, 16), quarter)]
-        return [remote(rows, rows, layer, 2 * parties, {"dp": 1 - chip})]
-
-    def spread_cores(layer):
-        rows = total.at[layer, pl.ds(pl.multiple_of(core * half_rows, 16), half_rows)]
-        return [remote(rows, rows, layer, 2 * parties + 1, {"sub": 1 - core})]
-
-    def begin(copies_of, layer):
-        for copy in copies_of(layer):
+    def spread_chips(stream):
+        rows = total.at[from_row(stream, mine, quarter)]
+        return [remote(rows, rows, stream, 2 * parties, {"dp": 1 - chip})]
+
+    def spread_cores(stream):
+        rows = total.at[from_row(stream, core * half_rows, half_rows)]
+        return [remote(rows, rows, stream, 2 * parties + 1, {"sub": 1 - core})]
+
+    def begin(copies_of, stream):
+        for copy in copies_of(stream):
             copy.start()
 
-    def finish(copies_of, layer):
-        for copy in copies_of(layer):
+    def finish(copies_of, stream):
+        for copy in copies_of(stream):
             copy.wait()
 
-    def sum_cores(layer):
-        finish(over_cores, layer)
-        own = part[layer, pl.ds(pl.multiple_of(core * half_rows, 16), half_rows)]
-        value = own + got_core[layer].astype(F32)
-        core_sum[layer] = value
-        core_sent[layer] = value.astype(BF16)
-        begin(over_chips, layer)
-
-    def sum_chips(layer):
-        finish(over_chips, layer)
-        own = core_sum[layer, pl.ds(pl.multiple_of(chip * quarter, 16), quarter)]
-        value = own + got_chip[layer].astype(F32)
-        chip_sum[layer] = value
-        chip_sent[layer] = value.astype(BF16)
-        begin(over_line, layer)
-
-    def sum_line(layer):
-        finish(over_line, layer)
-        value = chip_sum[layer, pl.ds(pl.multiple_of(me * share, 16), share)]
+    def sum_cores(stream):
+        finish(over_cores, stream)
+        own = part[from_row(stream, core * half_rows, half_rows)]
+        value = own + got_core[stream].astype(F32)
+        core_sum[stream] = value
+        core_sent[stream] = value.astype(BF16)
+        begin(over_chips, stream)
+
+    def sum_chips(stream):
+        finish(over_chips, stream)
+        own = core_sum[stream, pl.ds(pl.multiple_of(chip * quarter, 16), quarter)]
+        value = own + got_chip[stream].astype(F32)
+        chip_sum[stream] = value
+        chip_sent[stream] = value.astype(BF16)
+        begin(over_line, stream)
+
+    def sum_line(stream):
+        finish(over_line, stream)
+        value = chip_sum[stream, pl.ds(pl.multiple_of(me * share, 16), share)]
         for offset in range(1, parties):
-            value = value + got_line[layer, offset - 1].astype(F32)
+            value = value + got_line[stream, offset - 1].astype(F32)
         value = value * (1.0 / (4 * parties))
-        total[layer, pl.ds(pl.multiple_of(mine + me * share, 16), share)] = value.astype(BF16)
-        begin(spread_line, layer)
+        total[from_row(stream, mine + me * share, share)] = value.astype(BF16)
+        begin(spread_line, stream)
 
     def take_taps(weights, taken):
         square[:C, : TAPS * C] = weights[...].astype(F32)
@@ -387,12 +427,15 @@
 
     square[...] = jnp.zeros((LANES, TILES * LANES), F32)
     bias_kept[...] = jnp.zeros((2, 1, LANES), F32)
+    for number in (4, 5, 0):
+        bring(number).wait()
     bias_kept[0, :, :C] = bias_one[...]
     bias_kept[1, :, :C] = bias_two[...]
     live = mask_kept[...] > 0
     cells = dense(features)
     pl.semaphore_wait(barrier, len(partners))
     send(0, cells)
+    bring(2).wait()
     take_taps(weight_one, taken_one)
     arrive(0, cells, taps_one)
 
@@ -400,7 +443,9 @@
     pre_kept[...] = pre_one
     hidden = jnp.where(live, pre_one * jax.nn.sigmoid(pre_one), 0.0).astype(BF16)
     send(1, hidden)
+    bring(3).wait()
     take_taps(weight_two, taken_two)
+    bring(1).wait()
     upstream = dense(grad_out)
     turn_back(taken_two)
     arrive(1, hidden, taps_two)
@@ -410,37 +455,60 @@
     send(2, grad_two)
     activated = jnp.where(live, pre_two * jax.nn.sigmoid(pre_two), 0.0).astype(BF16)
     out_features[0] = sparse(activated)
+    leave(0).start()
     weight_grad(grad_two, taps_two, 0)
-    begin(over_cores, 0)
+    second, first = range(streams), range(streams, 2 * streams)
+    for stream in second:
+        begin(over_cores, stream)
     arrive(2, grad_two, taps_back)
-    sum_cores(0)
+    for stream in second:
+        sum_cores(stream)
 
     hidden_sum = convolve(taps_back, back[...])
     grad_one = jnp.where(live, hidden_sum * slope_of(pre_kept[...]), 0.0).astype(BF16)
     send(3, grad_one)
-    sum_chips(0)
+    for stream in second:
+        sum_chips(stream)
     turn_back(taken_one)
     weight_grad(grad_one, taps_one, 1)
-    begin(over_cores, 1)
-    sum_line(0)
-    sum_cores(1)
+    for stream in first:
+        begin(over_cores, stream)
+    for stream in second:
+        sum_line(stream)
+    for stream in first:
+        sum_cores(stream)
     arrive(3, grad_one, taps_back)
-    finish(spread_line, 0)
-    begin(spread_chips, 0)
-    sum_chips(1)
+    for stream in second:
+        finish(spread_line, stream)
+        begin(spread_chips, stream)
+    for stream in first:
+        sum_chips(stream)
     result = convolve(taps_back, back[...]).astype(BF16)
-    finish(spread_chips, 0)
-    begin(spread_cores, 0)
-    sum_line(1)
+    for stream in second:
+        finish(spread_chips, stream)
+        begin(spread_cores, stream)
+    for stream in first:
+        sum_line(stream)
     input_grad[0] = sparse(result)
-    finish(spread_line, 1)
-    begin(spread_chips, 1)
-    finish(spread_cores, 0)
+    leave(1).start()
+    for stream in first:
+        finish(spread_line, stream)
+        begin(spread_chips, stream)
+    for stream in second:
+        finish(spread_cores, stream)
     hand_out(0, weight_two_grad, bias_two_grad)
-    finish(spread_chips, 1)
-    begin(spread_cores, 1)
-    finish(spread_cores, 1)
+    leave(3).start()
+    leave(5).start()
+    for stream in first:
+        finish(spread_chips, stream)
+        begin(spread_cores, stream)
+    for stream in first:
+        finish(spread_cores, stream)
     hand_out(1, weight_one_grad, bias_one_grad)
+    leave(2).start()
+    leave(4).start()
+    for number in range(6):
+        leave(number).wait()
 
 
 def on_device(
@@ -448,20 +516,35 @@
 ):
     parties = lax.axis_size("blocks")
     sides = len(side_offsets(parties))
-    vmem = pl.BlockSpec(memory_space=pltpu.VMEM)
+    streams = stream_count(parties)
+    span = SUM_ROWS // streams
+    anywhere = pl.BlockSpec(memory_space=pl.ANY)
+    given = (
+        features,
+        grad_out,
+        weight_one,
+        weight_two,
+        bias_one[None],
+        bias_two[None],
+        heights,
+        counts,
+        neighbours,
+    )
+    out_shape = (
+        jax.ShapeDtypeStruct((1, C, ROWS), BF16),
+        jax.ShapeDtypeStruct((1, C, ROWS), BF16),
+        jax.ShapeDtypeStruct((C, TAPS * C), F32),
+        jax.ShapeDtypeStruct((C, TAPS * C), F32),
+        jax.ShapeDtypeStruct((1, C), F32),
+        jax.ShapeDtypeStruct((1, C), F32),
+    )
     results = pl.pallas_call(
         functools.partial(kernel, parties),
-        out_shape=(
-            jax.ShapeDtypeStruct((1, C, ROWS), BF16),
-            jax.ShapeDtypeStruct((1, C, ROWS), BF16),
-            jax.ShapeDtypeStruct((C, TAPS * C), F32),
-            jax.ShapeDtypeStruct((C, TAPS * C), F32),
-            jax.ShapeDtypeStruct((1, C), F32),
-            jax.ShapeDtypeStruct((1, C), F32),
-        ),
-        in_specs=[vmem] * 9,
-        out_specs=[vmem] * 6,
-        scratch_shapes=[
+        out_shape=out_shape,
+        in_specs=[anywhere] * 9,
+        out_specs=[anywhere] * 6,
+        scratch_shapes=[pltpu.VMEM(array.shape, array.dtype) for array in given + out_shape]
+        + [
             pltpu.VMEM((CELLS, ROWS), BF16),
             pltpu.VMEM((LEVELS * WIDE, LANES), BF16),
             pltpu.VMEM((LEVELS * WIDE, LANES), BF16),
@@ -477,39 +560,31 @@
             pltpu.VMEM((LEVELS + 2, WIDE, 3 * LANES), BF16),
             pltpu.VMEM((CELLS, LANES), F32),
             pltpu.VMEM((CELLS, LANES), F32),
-            pltpu.VMEM((4, 128, LANES), BF16),
-            pltpu.VMEM((4, 128, LANES), BF16),
-            pltpu.VMEM((4, sides, 128, LANES), BF16),
-            pltpu.VMEM((4, 128, LANES), BF16),
+            pltpu.VMEM((4, sides, 64, LANES), BF16),
+            pltpu.VMEM((4, 64, LANES), BF16),
+            pltpu.VMEM((4, sides, 64, LANES), BF16),
+            pltpu.VMEM((4, 64, LANES), BF16),
             pltpu.VMEM((2, SUM_ROWS, LANES), F32),
             pltpu.VMEM((2, SUM_ROWS, LANES), BF16),
-            pltpu.VMEM((2, SUM_ROWS // 2, LANES), BF16),
-            pltpu.VMEM((2, SUM_ROWS // 2, LANES), F32),
-            pltpu.VMEM((2, SUM_ROWS // 2, LANES), BF16),
-            pltpu.VMEM((2, SUM_ROWS // 4, LANES), BF16),
-            pltpu.VMEM((2, SUM_ROWS // 4, LANES), F32),
-            pltpu.VMEM((2, SUM_ROWS // 4, LANES), BF16),
-            pltpu.VMEM((2, parties - 1, SUM_ROWS // 4 // parties, LANES), BF16),
+            pltpu.VMEM((2 * streams, span // 2, LANES), BF16),
+            pltpu.VMEM((2 * streams, span // 2, LANES), F32),
+            pltpu.VMEM((2 * streams, span // 2, LANES), BF16),
+            pltpu.VMEM((2 * streams, span // 4, LANES), BF16),
+            pltpu.VMEM((2 * streams, span // 4, LANES), F32),
+            pltpu.VMEM((2 * streams, span // 4, LANES), BF16),
+            pltpu.VMEM((2 * streams, parties - 1, span // 4 // parties, LANES), BF16),
             pltpu.VMEM((2, SUM_ROWS, LANES), BF16),
             pltpu.SemaphoreType.DMA((4, sides + 1)),
             pltpu.SemaphoreType.DMA((4, sides + 1)),
-            pltpu.SemaphoreType.DMA((2, 2 * parties + 2)),
-            pltpu.SemaphoreType.DMA((2, 2 * parties + 2)),
+            pltpu.SemaphoreType.DMA((2 * streams, 2 * parties + 2)),
+            pltpu.SemaphoreType.DMA((2 * streams, 2 * parties + 2)),
+            pltpu.SemaphoreType.DMA((9,)),
+            pltpu.SemaphoreType.DMA((6,)),
         ],
         compiler_params=pltpu.CompilerParams(
-            collective_id=0, has_side_effects=True, vmem_limit_bytes=48 * 1024 * 1024
+            collective_id=0, has_side_effects=True, vmem_limit_bytes=60 * 1024 * 1024
         ),
-    )(
-        features,
-        grad_out,
-        weight_one,
-        weight_two,
-        bias_one[None],
-        bias_two[None],
-        heights,
-        counts,
-        neighbours,
-    )
+    )(*given)
     return (*results[:4], results[4][0], results[5][0])
 
 

time: 64.5 us -> 58.9 us (0.913)
  local copies, waits for them, and re-layouts: 10.1 us -> 6.63 us
  Pallas kernels: 53.3 us -> 51.4 us
    unnamed x24 -> x14, local copies, waits for them, and re-layouts: 10.1 us -> 6.63 us
    pallas_call x1, Pallas kernels: 53.3 us -> 51.4 us  [on_device(): pl.pallas_call(functools.partial(kernel, parties), out_shape=out_shape, i...]
where the time goes in v4:
time: 58.9 us; the launch traced here: 58.7 us
  Pallas kernels  51.4 us (87%)
  local copies, waits for them, and re-layouts  6.63 us (11%)
  between operations  0.66 us (1%)
    pallas_call x1, Pallas kernels, on_device(): pl.pallas_call(functools.partial(kernel, parties), out_shape=out_shape, i...  51.4 us
    unnamed x14, local copies, waits for them, and re-layouts  6.63 us

profile of v4, /device:TPU:0, one launch (start us, length us, event | category | flops | bytes accessed | tf_op | source)
XLA Modules:
  0.0 58.7 jit_solution(1969007392342187242)
XLA Ops:
  0.6 51.4 %shard_map.136 = (bf16[1,96,512]{2,1,0:T(8,128)(2,1)}, bf16[1,96,512]{2,1,0:T(8,128)(2,1)}, f32[96,2592]{1,0:T(8,128)}, f32[96,2592]{1,0:T(8,128)}, f32[1,96]{1,0:T(1,128)}, /*index=5*/f32[1,96]{1,0:T(1,128)}) custom-call(bf16[1,96,512]{2,1,0:T(8,128)(2,1)} %refs_0_.1, bf16[1,96,512]{2,1,0:T(8,128)(2,1)} %refs_1_.1, bf16[96,2592]{1,0:T(8,128)(2,1)} %refs_2_.1, ...), custom_call_target="tpu_custom_call" | custom-call | tf_op jit(solution)/shard_map/pallas_call | solution.py:541
  52.0 0.0 copy-start.1
  52.0 1.6 %copy.21 = bf16[1,96,512]{2,1,0:T(8,128)(2,1)} copy(bf16[1,96,512]{2,1,0:T(8,128)(2,1)} %get-tuple-element.24) | data formatting | bytes 196608
  53.6 0.0 copy-done.1
  53.6 0.6 %copy.22 = bf16[1,96,512]{2,1,0:T(8,128)(2,1)} copy(bf16[1,96,512]{2,1,0:T(8,128)(2,1)S(1)} %copy-done.1) | data formatting | bytes 196608
  54.3 0.0 copy-start
  54.3 2.3 %copy.23 = f32[96,2592]{1,0:T(8,128)} copy(f32[96,2592]{1,0:T(8,128)} %get-tuple-element.26) | data formatting | bytes 1990656
  56.6 0.0 copy-done
  56.6 0.0 copy-start.3
  56.6 1.0 %copy.24 = f32[96,2592]{1,0:T(8,128)} copy(f32[96,2592]{1,0:T(8,128)S(1)} %copy-done) | data formatting | bytes 1990656
  57.6 0.0 copy-done.3
  57.6 0.0 copy-start.2
  57.6 0.5 copy.25
  58.1 0.1 copy-done.2
  58.2 0.5 copy.26
Async XLA Ops:
  52.0 1.6 %copy-start.1 = (bf16[1,96,512]{2,1,0:T(8,128)(2,1)S(1)}, bf16[1,96,512]{2,1,0:T(8,128)(2,1)}, u32[]{:S(2)}) copy-start(bf16[1,96,512]{2,1,0:T(8,128)(2,1)} %get-tuple-element.25) | copy-start | bytes 294916
  54.3 2.3 %copy-start = (f32[96,2592]{1,0:T(8,128)S(1)}, f32[96,2592]{1,0:T(8,128)}, u32[]{:S(2)}) copy-start(f32[96,2592]{1,0:T(8,128)} %get-tuple-element.27) | copy-start | bytes 2985988
  56.6 1.0 %copy-start.3 = (f32[1,96]{1,0:T(1,128)S(1)}, f32[1,96]{1,0:T(1,128)}, u32[]{:S(2)}) copy-start(f32[1,96]{1,0:T(1,128)} %get-tuple-element.16) | copy-start | bytes 1156
  57.6 0.6 %copy-start.2 = (f32[1,96]{1,0:T(1,128)S(1)}, f32[1,96]{1,0:T(1,128)}, u32[]{:S(2)}) copy-start(f32[1,96]{1,0:T(1,128)} %get-tuple-element.17) | copy-start | bytes 1156

commit v5 on v4

--- a/solution.py
+++ b/solution.py
@@ -64,7 +64,6 @@
     given, refs = refs[:9], refs[9:]
     results, refs = refs[:6], refs[6:]
     held_in, refs = refs[:9], refs[9:]
-    held_out, refs = refs[:6], refs[6:]
     (
         features,
         grad_out,
@@ -83,7 +82,7 @@
         weight_two_grad,
         bias_one_grad,
         bias_two_grad,
-    ) = held_out
+    ) = results
     (
         place,
         spread_left,
@@ -119,14 +118,10 @@
         sum_send,
         sum_recv,
         in_sem,
-        out_sem,
     ) = refs
 
     def bring(number):
         return pltpu.make_async_copy(given[number], held_in[number], in_sem.at[number])
-
-    def leave(number):
-        return pltpu.make_async_copy(held_out[number], results[number], out_sem.at[number])
 
     for number in (6, 7, 8, 0, 2, 4, 5, 3, 1):
         bring(number).start()
@@ -160,32 +155,9 @@
         target = (low[slot : slot + 1] - LOW + layer) * PLANE + cell
         target = jnp.where(layer < held[slot : slot + 1], target, -1)
         place[:, slot * LANES : (slot + 1) * LANES] = one_hot(cell_at == target)
-    mask_kept[...] = dot(place[...], jnp.ones((ROWS, LANES), BF16))
-
-    row = iota((LEVELS * WIDE, LANES), 0)
-    level = row // WIDE
-    across = (row % WIDE) // EDGE
-    along = row % EDGE
-    wanted = jnp.where(
-        across == 0,
-        64 + level * EDGE + EDGE - 1,
-        jnp.where(across == EDGE + 1, 64 + level * EDGE, level * EDGE + across - 1),
-    )
-    lane = iota((LEVELS * WIDE, LANES), 1)
-    spread_left[...] = one_hot((along == 0) & (lane == wanted))
-    spread_right[...] = one_hot((along == EDGE - 1) & (lane == wanted))
     number = iota((128, CELLS), 0)
     spot = (number % 64) * EDGE + jnp.where(number >= 64, EDGE - 1, 0)
     pick[...] = one_hot(iota((128, CELLS), 1) == spot)
-
-    for taps in (taps_one, taps_two, taps_back):
-        taps[0] = jnp.zeros((WIDE, 3 * LANES), BF16)
-        taps[LEVELS + 1] = jnp.zeros((WIDE, 3 * LANES), BF16)
-
-    for layer in range(2):
-        spare = SUM_ROWS - TILES * C
-        part[layer, TILES * C :] = jnp.zeros((spare, LANES), F32)
-        part_sent[layer, TILES * C :] = jnp.zeros((spare, LANES), BF16)
 
     def dense(rows_ref):
         padded = jnp.concatenate([rows_ref[0], jnp.zeros((LANES - C, ROWS), BF16)], axis=0)
@@ -241,6 +213,18 @@
     up, down, left, right = there(0, 1), there(2, 0), there(0, 3), there(1, 2)
 
     def arrive(turn, cells, taps):
+        along = iota((PLANE, LANES), 0) % EDGE
+
+        def shifted(values):
+            rows = values.shape[0]
+            at = along[:rows]
+            return (
+                jnp.where(at == 0, 0.0, pltpu.roll(values, 1, 0)),
+                values,
+                jnp.where(at == EDGE - 1, 0.0, pltpu.roll(values, rows - 1, 0)),
+            )
+
+        own = [shifted(cells[z * PLANE : (z + 1) * PLANE].astype(F32)) for z in range(LEVELS)]
         for copy in copies(turn):
             copy.wait()
         inside = iota((64, LANES), 0) % EDGE
@@ -260,16 +244,12 @@
 
         from_left = columns(1, (half + 1) % parties, left)
         from_right = columns(parties - 1, (half - 1) % parties, right)
-        pieces = []
+        pieces = [[], [], []]
         for z in range(LEVELS):
-            beside = got_across[turn, z * EDGE : (z + 1) * EDGE].astype(F32)
-            pieces.append(jnp.where(up, beside, 0.0))
-            pieces.append(cells[z * PLANE : (z + 1) * PLANE].astype(F32))
-            pieces.append(jnp.where(down, beside, 0.0))
-        middle = jnp.concatenate(pieces, axis=0)
-        place_along = iota((LEVELS * WIDE, LANES), 0) % EDGE
-        before = jnp.where(place_along == 0, 0.0, pltpu.roll(middle, 1, 0))
-        after = jnp.where(place_along == EDGE - 1, 0.0, pltpu.roll(middle, LEVELS * WIDE - 1, 0))
+            beside = shifted(got_across[turn, z * EDGE : (z + 1) * EDGE].astype(F32))
+            for part, outer, inner in zip(pieces, beside, own[z]):
+                part += [jnp.where(up, outer, 0.0), inner, jnp.where(down, outer, 0.0)]
+        before, middle, after = [jnp.concatenate(part, axis=0) for part in pieces]
         before = (before + dot(spread_left[...], from_left)).astype(BF16)
         after = (after + dot(spread_right[...], from_right)).astype(BF16)
         middle = middle.astype(BF16)
@@ -425,16 +405,38 @@
         weights_out[:, (TILES - 1) * LANES :] = last[:C, :rest]
         bias_out[...] = jnp.transpose(last)[rest : rest + 1, :C]
 
+    bring(0).wait()
+    cells = dense(features)
+    pl.semaphore_wait(barrier, len(partners))
+    send(0, cells)
+    mask_kept[...] = dot(place[...], jnp.ones((ROWS, LANES), BF16))
+    live = mask_kept[...] > 0
+    row = iota((LEVELS * WIDE, LANES), 0)
+    level = row // WIDE
+    across = (row % WIDE) // EDGE
+    along = row % EDGE
+    wanted = jnp.where(
+        across == 0,
+        64 + level * EDGE + EDGE - 1,
+        jnp.where(across == EDGE + 1, 64 + level * EDGE, level * EDGE + across - 1),
+    )
+    lane = iota((LEVELS * WIDE, LANES), 1)
+    spread_left[...] = one_hot((along == 0) & (lane == wanted))
+    spread_right[...] = one_hot((along == EDGE - 1) & (lane == wanted))
+    for taps in (taps_one, taps_two, taps_back):
+        taps[0] = jnp.zeros((WIDE, 3 * LANES), BF16)
+        taps[LEVELS + 1] = jnp.zeros((WIDE, 3 * LANES), BF16)
+
+    for layer in range(2):
+        spare = SUM_ROWS - TILES * C
+        part[layer, TILES * C :] = jnp.zeros((spare, LANES), F32)
+        part_sent[layer, TILES * C :] = jnp.zeros((spare, LANES), BF16)
     square[...] = jnp.zeros((LANES, TILES * LANES), F32)
     bias_kept[...] = jnp.zeros((2, 1, LANES), F32)
-    for number in (4, 5, 0):
+    for number in (4, 5):
         bring(number).wait()
     bias_kept[0, :, :C] = bias_one[...]
     bias_kept[1, :, :C] = bias_two[...]
-    live = mask_kept[...] > 0
-    cells = dense(features)
-    pl.semaphore_wait(barrier, len(partners))
-    send(0, cells)
     bring(2).wait()
     take_taps(weight_one, taken_one)
     arrive(0, cells, taps_one)
@@ -455,7 +457,6 @@
     send(2, grad_two)
     activated = jnp.where(live, pre_two * jax.nn.sigmoid(pre_two), 0.0).astype(BF16)
     out_features[0] = sparse(activated)
-    leave(0).start()
     weight_grad(grad_two, taps_two, 0)
     second, first = range(streams), range(streams, 2 * streams)
     for stream in second:
@@ -490,25 +491,18 @@
     for stream in first:
         sum_line(stream)
     input_grad[0] = sparse(result)
-    leave(1).start()
     for stream in first:
         finish(spread_line, stream)
         begin(spread_chips, stream)
     for stream in second:
         finish(spread_cores, stream)
     hand_out(0, weight_two_grad, bias_two_grad)
-    leave(3).start()
-    leave(5).start()
     for stream in first:
         finish(spread_chips, stream)
         begin(spread_cores, stream)
     for stream in first:
         finish(spread_cores, stream)
     hand_out(1, weight_one_grad, bias_one_grad)
-    leave(2).start()
-    leave(4).start()
-    for number in range(6):
-        leave(number).wait()
 
 
 def on_device(
@@ -542,8 +536,8 @@
         functools.partial(kernel, parties),
         out_shape=out_shape,
         in_specs=[anywhere] * 9,
-        out_specs=[anywhere] * 6,
-        scratch_shapes=[pltpu.VMEM(array.shape, array.dtype) for array in given + out_shape]
+        out_specs=[pl.BlockSpec(memory_space=pltpu.VMEM)] * 6,
+        scratch_shapes=[pltpu.VMEM(array.shape, array.dtype) for array in given]
         + [
             pltpu.VMEM((CELLS, ROWS), BF16),
             pltpu.VMEM((LEVELS * WIDE, LANES), BF16),
@@ -579,7 +573,6 @@
             pltpu.SemaphoreType.DMA((2 * streams, 2 * parties + 2)),
             pltpu.SemaphoreType.DMA((2 * streams, 2 * parties + 2)),
             pltpu.SemaphoreType.DMA((9,)),
-            pltpu.SemaphoreType.DMA((6,)),
         ],
         compiler_params=pltpu.CompilerParams(
             collective_id=0, has_side_effects=True, vmem_limit_bytes=60 * 1024 * 1024

time: 58.9 us -> 58.4 us (level)
  no operation moved by 1% of the time
where the time goes in v5:
time: 58.4 us; the launch traced here: 58.2 us
  Pallas kernels  51 us (87%)
  local copies, waits for them, and re-layouts  6.63 us (11%)
  between operations  0.66 us (1%)
    pallas_call x1, Pallas kernels, on_device(): pl.pallas_call(functools.partial(kernel, parties), out_shape=out_shape, i...  51 us
    unnamed x14, local copies, waits for them, and re-layouts  6.63 us

profile of v5, /device:TPU:0, one launch (start us, length us, event | category | flops | bytes accessed | tf_op | source)
XLA Modules:
  0.0 58.2 jit_solution(8782865054023395094)
XLA Ops:
  0.6 51.0 %shard_map.136 = (bf16[1,96,512]{2,1,0:T(8,128)(2,1)}, bf16[1,96,512]{2,1,0:T(8,128)(2,1)}, f32[96,2592]{1,0:T(8,128)}, f32[96,2592]{1,0:T(8,128)}, f32[1,96]{1,0:T(1,128)}, /*index=5*/f32[1,96]{1,0:T(1,128)}) custom-call(bf16[1,96,512]{2,1,0:T(8,128)(2,1)} %refs_0_.1, bf16[1,96,512]{2,1,0:T(8,128)(2,1)} %refs_1_.1, bf16[96,2592]{1,0:T(8,128)(2,1)} %refs_2_.1, ...), custom_call_target="tpu_custom_call" | custom-call | tf_op jit(solution)/shard_map/pallas_call | solution.py:535
  51.6 0.0 copy-start.1
  51.6 1.6 %copy.21 = bf16[1,96,512]{2,1,0:T(8,128)(2,1)} copy(bf16[1,96,512]{2,1,0:T(8,128)(2,1)} %get-tuple-element.24) | data formatting | bytes 196608
  53.2 0.0 copy-done.1
  53.2 0.6 %copy.22 = bf16[1,96,512]{2,1,0:T(8,128)(2,1)} copy(bf16[1,96,512]{2,1,0:T(8,128)(2,1)S(1)} %copy-done.1) | data formatting | bytes 196608
  53.8 0.0 copy-start
  53.8 2.3 %copy.23 = f32[96,2592]{1,0:T(8,128)} copy(f32[96,2592]{1,0:T(8,128)} %get-tuple-element.26) | data formatting | bytes 1990656
  56.2 0.0 copy-done
  56.2 0.0 copy-start.3
  56.2 1.0 %copy.24 = f32[96,2592]{1,0:T(8,128)} copy(f32[96,2592]{1,0:T(8,128)S(1)} %copy-done) | data formatting | bytes 1990656
  57.1 0.0 copy-done.3
  57.1 0.0 copy-start.2
  57.1 0.5 copy.25
  57.6 0.1 copy-done.2
  57.7 0.5 copy.26
Async XLA Ops:
  51.6 1.6 %copy-start.1 = (bf16[1,96,512]{2,1,0:T(8,128)(2,1)S(1)}, bf16[1,96,512]{2,1,0:T(8,128)(2,1)}, u32[]{:S(2)}) copy-start(bf16[1,96,512]{2,1,0:T(8,128)(2,1)} %get-tuple-element.25) | copy-start | bytes 294916
  53.8 2.3 %copy-start = (f32[96,2592]{1,0:T(8,128)S(1)}, f32[96,2592]{1,0:T(8,128)}, u32[]{:S(2)}) copy-start(f32[96,2592]{1,0:T(8,128)} %get-tuple-element.27) | copy-start | bytes 2985988
  56.2 1.0 %copy-start.3 = (f32[1,96]{1,0:T(1,128)S(1)}, f32[1,96]{1,0:T(1,128)}, u32[]{:S(2)}) copy-start(f32[1,96]{1,0:T(1,128)} %get-tuple-element.16) | copy-start | bytes 1156
  57.1 0.6 %copy-start.2 = (f32[1,96]{1,0:T(1,128)S(1)}, f32[1,96]{1,0:T(1,128)}, u32[]{:S(2)}) copy-start(f32[1,96]{1,0:T(1,128)} %get-tuple-element.17) | copy-start | bytes 1156
